TPU v7x, 32 devices: a whole 2x2x4 slice. The times are simulated.
32 devices in a mesh: view: 4 (over x, core), block: 8 (over z, y).
Axes of the slice: x: 2, y: 2, z: 4, core: 2. Of those that a mesh axis runs over, the one named last changes fastest.
Arguments:
- estimate: float32 [8, 8, 128], P('block'), may hold values from 0.5 to 2
- view_data: float32 [4, 16, 8, 1, 128], P('view', 'block'), may hold values from 0.5 to 2
- taps_x: float32 [4, 33], P('view'), may hold values from 0.05 to 1
- taps_y: float32 [4, 33], P('view'), may hold values from 0.05 to 1
- taps_z: float32 [4, 33], P('view'), may hold values from 0.05 to 1
- owner: int32 [4, 8, 1], P('view'), may hold values from 0 to 7; in each aligned block of 8 rows (0 to 7, 8 to 15, ..., all dimensions but the last counted through in order) at most 2 rows name the same one
Outputs:
- joined: float32 [8, 8, 128], P('block')
Inputs may be any that keep to these rules, and one draw needn't show every extreme that they name: `owner`: each view gives at most 2 slabs to one device, and some device holds 2 slabs of some view.
All inputs are finite; a program needn't handle non-finite values.
Results may differ from a plain program's by a relative error of at most 0.0001.
Values sent between devices are 32-bit elements; how exact they have to be, the bound alone decides.
No kernel may reach another device: no remote copies, remote signals or barrier semaphores. Data moves between devices by JAX's collectives and lax.ppermute only.
A program may use at most 64 MiB of HBM per device.

v0:
```python
import jax
import jax.numpy as jnp
from jax import lax
from jax.sharding import PartitionSpec as P

ITERS = 2


HIGH = lax.Precision.HIGHEST


def band_matrix(taps, length):
    width = taps.shape[0]
    reach = width // 2
    rows = jnp.arange(length, dtype=jnp.int32)[:, None]
    cols = jnp.arange(length, dtype=jnp.int32)[None, :]
    offset = cols - rows + reach
    inside = (offset >= 0) & (offset < width)
    index = jnp.clip(offset, 0, width - 1)
    values = jnp.take(taps, index.reshape(-1), axis=0).reshape(length, length)
    return jnp.where(inside, values, jnp.zeros_like(values))


def on_device(estimate, view_data, taps_x, taps_y, taps_z, owner):
    blocks = lax.axis_size("block")
    views = lax.axis_size("view")
    thin = estimate.shape[0]
    total_y = estimate.shape[1]
    depth = estimate.shape[2]
    total_x = thin * blocks
    slots = view_data.shape[1]
    own = owner[0, :, 0]
    order = jnp.arange(blocks, dtype=jnp.int32)
    earlier = (own[:, None] == own[None, :]) & (order[None, :] < order[:, None])
    place = jnp.sum(earlier.astype(jnp.int32), axis=1)
    slot_ids = jnp.arange(slots, dtype=jnp.int32)
    hits = (place[None, None, :] == slot_ids[:, None, None]) & (
        own[None, None, :] == order[None, :, None]
    )
    filled = jnp.any(hits, axis=2).astype(jnp.float32)
    source_slab = jnp.sum(jnp.where(hits, order[None, None, :], 0), axis=2)
    return_index = place * blocks + own
    device = lax.axis_index("block")
    held = jnp.sum((own == device).astype(jnp.int32))
    live = (slot_ids < held)[:, None, None, None]
    m_x = band_matrix(taps_x[0], total_x)
    m_y = band_matrix(taps_y[0], total_y)
    m_z = band_matrix(taps_z[0], depth)
    recorded = view_data[0]
    est = estimate
    for step in range(ITERS):
        forward = jnp.einsum("ij,xjz->xiz", m_y, est, precision=HIGH)
        pieces = forward.reshape(thin, blocks, thin, depth)
        picked = jnp.take(pieces, source_slab.reshape(-1), axis=1)
        picked = picked.reshape(thin, slots, blocks, thin, depth).transpose(1, 2, 0, 3, 4)
        picked = picked * filled[:, :, None, None, None]
        arrived = lax.all_to_all(picked, "block", split_axis=1, concat_axis=1, tiled=True)
        held_est = arrived.reshape(slots, total_x, thin, depth)
        blurred = jnp.einsum("ij,sjyz->siyz", m_x, held_est, precision=HIGH)
        blurred = jnp.einsum("sxyj,ij->sxyi", blurred, m_z, precision=HIGH)
        ratio = jnp.where(live, recorded / jnp.where(live, blurred, 1.0), 0.0)
        back = jnp.einsum("ji,sjyz->siyz", m_x, ratio, precision=HIGH)
        back = jnp.einsum("sxyj,ji->sxyi", back, m_z, precision=HIGH)
        returned = lax.all_to_all(
            back.reshape(slots, blocks, thin, thin, depth),
            "block",
            split_axis=1,
            concat_axis=1,
            tiled=True,
        )
        flat = returned.reshape(slots * blocks, thin, thin, depth)
        gathered = jnp.take(flat, return_index, axis=0)
        corr = gathered.transpose(1, 0, 2, 3).reshape(thin, total_y, depth)
        corr = jnp.einsum("ji,xjz->xiz", m_y, corr, precision=HIGH)
        logs = lax.psum(jnp.log(corr), "view")
        est = est * jnp.exp(logs / views)
    return est


def solution(mesh):
    in_specs = (
        P("block", None, None),
        P("view", "block", None, None, None),
        P("view", None),
        P("view", None),
        P("view", None),
        P("view", None, None),
    )
    out_specs = P("block", None, None)
    return jax.shard_map(
        on_device, mesh=mesh, in_specs=in_specs, out_specs=out_specs, check_vma=False
    )
```

profile of v0, /device:TPU:0, one launch (start us, length us, event | category | flops | bytes accessed | tf_op | source)
XLA Modules:
  0.0 90.1 jit_solution(14173759529747401455)
XLA Ops:
  0.0 0.6 copy-done.5
  0.7 0.2 convert_reduce_fusion
  0.9 0.1 fusion.16
  1.0 0.1 reshape.401
  1.1 0.1 and_reduce_fusion
  1.3 0.1 min.34
  1.4 0.8 gather_fusion
  2.2 0.7 copy-done.1
  2.8 0.8 gather_fusion.2
  3.6 0.1 and.101
  3.7 0.1 select_n.163
  3.8 0.1 copy.21
  3.9 0.6 copy-done.3
  4.5 0.1 fusion.28
  4.6 0.6 gather_fusion.1
  5.3 0.7 copy_multiply_fusion.1
  5.9 7.4 %all-to-all-start = ((f32[2,8,1,1,128]{4,0,3,2,1:T(2,128)}), f32[2,8,1,1,128]{4,0,3,2,1:T(2,128)S(1)}, u32[]{:S(2)}, u32[]{:S(2)}) async-start(f32[2,8,1,1,128]{4,0,3,2,1:T(2,128)} %copy_multiply_fusion.1), calls=%async_computation | async-start | bytes 16384 | tf_op jit(solution)/shard_map/all_to_all | solution.py:57
  13.4 0.7 fusion.43
  14.1 0.7 fusion.44
  14.8 4.8 %compare_select_fusion.1 = (f32[16384,1]{0,1:T(1,128)S(1)}, s32[16384,1]{0,1:T(1,128)S(1)}) fusion(f32[]{:T(128)} %bitcast.45, f32[]{:T(128)} %bitcast.46, f32[]{:T(128)} %bitcast.47, f32[]{:T(128)} %bitcast.48, f32[]{:T(128)} %bitcast.49, f32[]{:T(128)} %bitcast.51, f32[]{:T(128)} %bitcast.50, s32[16384,1]{0,1:T(1,128)S(1)} %bitcast.185), kind=kLoop, calls=%fused_computation.50 | loop fusion | flops 245760 | bytes 196636 | tf_op jit(solution)/shard_map/jit(_take)/gather | solution.py:20
  19.6 5.2 %compare_reduce_fusion.25 = (pred[16384]{0:T(1024)(128)(4,1)S(1)}, pred[16384]{0:T(1024)(128)(4,1)S(1)}, pred[16384]{0:T(1024)(128)(4,1)S(1)}, pred[16384]{0:T(1...) fusion(s32[16384,1]{0,1:T(1,128)S(1)} %get-tuple-element.37), kind=kLoop, calls=%fused_computation.49 | loop fusion | flops 425984 | bytes 491520 | tf_op jit(solution)/shard_map/jit(_take)/gather | solution.py:20
  24.9 0.7 fusion.39
  25.6 16.4 %fusion.10 = f32[16384]{0:T(1024)S(1)} fusion(pred[16384]{0:T(1024)(128)(4,1)S(1)} %get-tuple-element.33, pred[16384]{0:T(1024)(128)(4,1)S(1)} %get-tuple-element.32, pred[16384]{0:T(1024)(128)(4,1)S(1)} %get-tuple-element.31, pred[16384]{0:T(1024)(128)(4,1)S(1)} %get-tuple-element.30, pred[16384]{0:T(1024)(128)(4,1)S(1)} %get-tuple-element.29, ...), kind=kLoop, calls=%fused_computation.62 | loop fusion | flops 655360 | bytes 557160 | tf_op jit(solution)/shard_map/jit(_where)/select_n | solution.py:21
  42.0 0.7 iota_compare_fusion.3
  42.7 0.1 reshape.701
  42.8 0.1 convolution_bitcast_fusion.5
  43.0 0.6 copy-done.4
  43.5 0.2 fusion.3
  43.8 0.2 convolution_bitcast_fusion.4
  44.0 0.2 convolution_bitcast_fusion.3
  44.1 0.6 copy.25
  44.7 6.0 %all-to-all-start.1 = ((f32[2,8,1,1,128]{4,0,3,2,1:T(2,128)}), f32[2,8,1,1,128]{4,0,3,2,1:T(2,128)S(1)}, u32[]{:S(2)}, u32[]{:S(2)}) async-start(f32[2,8,1,1,128]{4,0,3,2,1:T(2,128)} %copy.25), calls=%async_computation.1 | async-start | bytes 16384 | tf_op jit(solution)/shard_map/all_to_all | solution.py:64
  50.7 6.5 %all-to-all-done.1 = f32[2,8,1,1,128]{4,0,3,2,1:T(2,128)S(1)} async-done(((f32[2,8,1,1,128]{4,0,3,2,1:T(2,128)}), f32[2,8,1,1,128]{4,0,3,2,1:T(2,128)S(1)}, u32[]{:S(2)}, u32[]{:S(2)}) %all-to-all-start.1) | async-done | bytes 8224 | tf_op jit(solution)/shard_map/all_to_all | solution.py:64
  57.3 0.6 gather_fusion.3
  57.8 0.2 fusion.5
  58.0 5.7 %psum.14 = f32[1,8,128]{2,1,0:T(8,128)S(1)} all-reduce(f32[1,8,128]{2,1,0:T(8,128)S(1)} %fusion.5), channel_id=1, replica_groups=mesh['view'=4,'block'=8] {'view'}, use_global_device_ids=true, to_apply=%region_4.0 | all-reduce | flops 1024 | bytes 8192 | tf_op jit(solution)/shard_map/psum | solution.py:75
  63.7 0.1 convolution_bitcast_fusion.6
  63.8 0.6 gather_fusion.4
  64.5 8.9 %all_to_all.20 = f32[2,8,1,1,128]{4,0,3,2,1:T(2,128)S(1)} all-to-all(f32[2,8,1,1,128]{4,0,3,2,1:T(2,128)S(1)} %copy_multiply_fusion), channel_id=1, replica_groups=mesh['view'=4,'block'=8] {'block'}, dimensions={1} | all-to-all | bytes 16384 | tf_op jit(solution)/shard_map/all_to_all | solution.py:57
  73.4 0.1 convolution_bitcast_fusion.2
  73.5 0.2 fusion.1
  73.8 0.2 convolution_bitcast_fusion.1
  74.0 0.2 convolution_bitcast_fusion
  74.1 8.9 %all_to_all.21 = f32[2,8,1,1,128]{4,0,3,2,1:T(2,128)S(1)} all-to-all(f32[2,8,1,1,128]{4,0,3,2,1:T(2,128)S(1)} %copy.30), channel_id=1, replica_groups=mesh['view'=4,'block'=8] {'block'}, dimensions={1} | all-to-all | bytes 16384 | tf_op jit(solution)/shard_map/all_to_all | solution.py:64
  83.0 0.6 gather_fusion.5
  83.6 0.2 fusion.4
  83.8 5.7 %psum.15 = f32[1,8,128]{2,1,0:T(8,128)S(1)} all-reduce(f32[1,8,128]{2,1,0:T(8,128)S(1)} %fusion.4), channel_id=1, replica_groups=mesh['view'=4,'block'=8] {'view'}, use_global_device_ids=true, to_apply=%region_5.9 | all-reduce | flops 1024 | bytes 8192 | tf_op jit(solution)/shard_map/psum | solution.py:75
  89.4 0.6 exponential_multiply_fusion
  (30 shorter events, 0.5 us)
Async XLA Ops:
  0.0 1.4 %copy-start = (f32[1,33]{1,0:T(1,128)S(1)}, f32[1,33]{1,0:T(1,128)}, u32[]{:S(2)}) copy-start(f32[1,33]{1,0:T(1,128)} %param.15) | copy-start | bytes 400
  0.0 0.7 copy-start.5
  2.2 0.7 copy-start.1
  3.8 0.7 copy-start.3
  5.9 7.4 %copy-start.2 = (f32[1,33]{1,0:T(1,128)S(1)}, f32[1,33]{1,0:T(1,128)}, u32[]{:S(2)}) copy-start(f32[1,33]{1,0:T(1,128)} %param.16) | copy-start | bytes 400
  5.9 36.9 %all-to-all-start = ((f32[2,8,1,1,128]{4,0,3,2,1:T(2,128)}), f32[2,8,1,1,128]{4,0,3,2,1:T(2,128)S(1)}, u32[]{:S(2)}, u32[]{:S(2)}) async-start(f32[2,8,1,1,128]{4,0,3,2,1:T(2,128)} %copy_multiply_fusion.1), calls=%async_computation | async-start | bytes 16384 | tf_op jit(solution)/shard_map/all_to_all | solution.py:57
  42.8 0.7 copy-start.4
  44.7 12.5 %all-to-all-start.1 = ((f32[2,8,1,1,128]{4,0,3,2,1:T(2,128)}), f32[2,8,1,1,128]{4,0,3,2,1:T(2,128)S(1)}, u32[]{:S(2)}, u32[]{:S(2)}) async-start(f32[2,8,1,1,128]{4,0,3,2,1:T(2,128)} %copy.25), calls=%async_computation.1 | async-start | bytes 16384 | tf_op jit(solution)/shard_map/all_to_all | solution.py:64
where the time goes:
time: 90.8 us; the launch traced here: 90.1 us
  other arithmetic  29.9 us (33%)
  blocking collectives  29.1 us (32%)
  starting transfers between devices  13.4 us (15%)
  local copies, waits for them, and re-layouts  8.93 us (10%)
  waiting for transfers between devices  6.51 us (7%)
  matrix products  1.99 us (2%)
    select_n x2, other arithmetic, band_matrix(): return jnp.where(inside, values, jnp.zeros_like(values))  16.4 us
    psum x2, blocking collectives, on_device(): logs = lax.psum(jnp.log(corr), 'view')  11.3 us
    gather x2, other arithmetic, band_matrix(): values = jnp.take(taps, index.reshape(-1), axis=0).reshape(length, length)  10 us
    all_to_all x1, blocking collectives, on_device(): lax.all_to_all(back.reshape(slots, blocks, thin, thin, depth), 'block', s...  8.88 us
    all_to_all x1, blocking collectives, on_device(): lax.all_to_all(picked, 'block', split_axis=1, concat_axis=1, tiled=True)  8.87 us
    all_to_all x1, starting transfers between devices, on_device(): lax.all_to_all(picked, 'block', split_axis=1, concat_axis=1, tiled=True)  7.42 us
    all_to_all x1, waiting for transfers between devices, on_device(): lax.all_to_all(back.reshape(slots, blocks, thin, thin, depth), 'block', s...  6.51 us
    all_to_all x1, starting transfers between devices, on_device(): lax.all_to_all(back.reshape(slots, blocks, thin, thin, depth), 'block', s...  5.99 us
  transfers between devices with their start and end apart: 2, of which 1 were waited for; matrix products, arithmetic and copies ran while one was open for 33% of the time, Pallas kernels for 0%

commit v1 on v0

--- a/solution.py
+++ b/solution.py
@@ -1,12 +1,204 @@
+import functools
+
 import jax
 import jax.numpy as jnp
 from jax import lax
+from jax.experimental import pallas as pl
+from jax.experimental.pallas import tpu as pltpu
 from jax.sharding import PartitionSpec as P
 
 ITERS = 2
 
-
 HIGH = lax.Precision.HIGHEST
+
+SIDE = 8
+LANES = 128
+DATA_ROWS = 16
+PACKET = 24
+
+
+def lane_ids(rows):
+    return lax.broadcasted_iota(jnp.int32, (rows, LANES), 1)
+
+
+def row_ids(rows):
+    return lax.broadcasted_iota(jnp.int32, (rows, LANES), 0)
+
+
+def pack_kernel(copies, reach, own, est, data, tx, ty, tz, out, taps):
+    block = lax.axis_index("block")
+    view = lax.axis_index("view")
+    width = 2 * reach + 1
+    taps[...] = jnp.zeros_like(taps)
+    taps[2:3, :width] = tz[...]
+    taps[3:4, :width] = tx[...]
+    taps[4:5, :width] = tx[...]
+    taps[5:6, :width] = ty[...]
+    first = jnp.int32(-1)
+    second = jnp.int32(-1)
+    for y in range(SIDE):
+        mine = own[y] == block
+        second = jnp.where(mine & (first >= 0), y, second)
+        first = jnp.where(mine & (first < 0), y, first)
+    lane = lane_ids(SIDE)
+    row = row_ids(SIDE)
+    along_z = jnp.where(lane < LANES // 2, lane, lane - LANES) + reach
+    along_x = (lane & (SIDE - 1)) + reach
+    along_y = (lane >> 3) + jnp.where(lane < LANES // 2, reach, reach - 16)
+    index = jnp.where(row == 2, along_z, jnp.where(row == 3, along_x, jnp.where(row == 4, along_x - SIDE, along_y)))
+    inside = (index >= 0) & (index < width)
+    picked = jnp.take_along_axis(taps[...], jnp.clip(index, 0, width - 1), axis=1)
+    tile = jnp.where(inside, picked, 0.0)
+    for k in range(2):
+        tile = jnp.where(row == k, est[pl.ds(2 * view + k, 1), :], tile)
+    tile = jnp.where(row == 6, first.astype(jnp.float32), tile)
+    tile = jnp.where(row == 7, second.astype(jnp.float32), tile)
+    lower, upper = data[:SIDE], data[SIDE:]
+    for k in range(copies):
+        out[k, :SIDE] = lower
+        out[k, SIDE:DATA_ROWS] = upper
+        out[k, DATA_ROWS:] = tile
+
+
+def halves(value):
+    high = value.astype(jnp.bfloat16)
+    low = (value - high.astype(jnp.float32)).astype(jnp.bfloat16)
+    return high, low
+
+
+def matmul(a, b):
+    return jnp.dot(a, b, preferred_element_type=jnp.float32)
+
+
+def per_side(matrix):
+    doubled = jnp.concatenate([matrix, matrix], axis=1)
+    high, low = halves(doubled)
+    both = jnp.where(lane_ids(matrix.shape[0]) < matrix.shape[1], high.astype(jnp.float32), low.astype(jnp.float32))
+    both = both.astype(jnp.bfloat16)
+    return jnp.concatenate([both, both], axis=1)
+
+
+def per_depth(matrix):
+    high, low = halves(matrix)
+    row = jnp.concatenate([high, low], axis=1)
+    return jnp.concatenate([row, row], axis=0)
+
+
+def apply_side(sided, value):
+    high, low = halves(value)
+    return matmul(sided, jnp.concatenate([high, high, low, low], axis=0))
+
+
+def apply_depth(value, deep):
+    high, low = halves(value)
+    both = matmul(jnp.concatenate([high, low], axis=1), deep)
+    return both[:, :LANES] + both[:, LANES:]
+
+
+def geometric_mean(values):
+    if len(values) == 1:
+        return values[0]
+    half = len(values) // 2
+    return jnp.sqrt(geometric_mean(values[:half]) * geometric_mean(values[half:]))
+
+
+def volume_kernel(blocks, groups, reach, near, far, out, held):
+    block = lax.axis_index("block")
+    core = lax.axis_index("view") & 1
+    sources = [(ref, g * blocks * PACKET) for ref in (near, far) for g in range(groups)]
+
+    tiles = []
+    for y in range(SIDE):
+        view, k = y // 2, y % 2
+        start = (view // 2) * blocks * PACKET + DATA_ROWS + k
+        rows = pl.ds(start, blocks, stride=PACKET)
+        same = (core == view % 2).astype(jnp.int32) > 0
+        tiles.append(jnp.where(same, near[rows, :], far[rows, :]))
+    est = jnp.concatenate(tiles, axis=0)
+
+    lane, row = lane_ids(SIDE), row_ids(SIDE)
+    band = jnp.abs(lane_ids(LANES) - row_ids(LANES)) <= reach
+    recorded, forward_side, forward_depth, back_side, back_depth = [], [], [], [], []
+    for ref, start in sources:
+        slabs = [jnp.zeros((SIDE, LANES), jnp.float32)] * SIDE
+        for b in range(blocks):
+            at = start + b * PACKET
+            for s in range(2):
+                label = jnp.broadcast_to(ref[at + DATA_ROWS + 6 + s : at + DATA_ROWS + 7 + s, :], (SIDE, LANES))
+                slab = ref[at + s * SIDE : at + (s + 1) * SIDE, :]
+                for y in range(SIDE):
+                    slabs[y] = jnp.where(label == y, slab, slabs[y])
+        recorded.append(jnp.concatenate(slabs, axis=0))
+
+        def meta(k, rows):
+            at = start + DATA_ROWS + k
+            return jnp.broadcast_to(ref[at : at + 1, :], (rows, LANES))
+
+        deep = pltpu.roll(meta(2, LANES), 0, 1, stride=1, stride_axis=0)
+        deep = jnp.where(band, deep, 0.0)
+        forward_depth.append(per_depth(deep.T))
+        back_depth.append(per_depth(deep))
+        upper = pltpu.roll(meta(3, SIDE), 0, 1, stride=1, stride_axis=0)
+        lower = pltpu.roll(meta(4, SIDE), 0, 1, stride=1, stride_axis=0)
+        x_tile = jnp.where((lane & (SIDE - 1)) >= row, upper, lower)
+        y_tile = pltpu.roll(meta(5, SIDE), 0, 1, stride=SIDE, stride_axis=0)
+        side = jnp.concatenate([x_tile * y_tile[y : y + 1, :] for y in range(SIDE)], axis=0)
+        side = side[:, : SIDE * SIDE]
+        forward_side.append(per_side(side))
+        back_side.append(per_side(side.T))
+
+    for step in range(ITERS):
+        corrections = []
+        for v in range(len(sources)):
+            blurred = apply_side(forward_side[v], apply_depth(est, forward_depth[v]))
+            ratio = recorded[v] / blurred
+            corrections.append(apply_depth(apply_side(back_side[v], ratio), back_depth[v]))
+        est = est * geometric_mean(corrections)
+    held[...] = est
+    out[...] = held[pl.ds(block, SIDE, stride=SIDE), :]
+
+
+def on_device_small(estimate, view_data, taps_x, taps_y, taps_z, owner):
+    blocks = lax.axis_size("block")
+    views = lax.axis_size("view")
+    reach = taps_x.shape[1] // 2
+    groups = views // 2
+    copies = groups * blocks
+    smem = pl.BlockSpec(memory_space=pltpu.SMEM)
+    vmem = pl.BlockSpec(memory_space=pltpu.VMEM)
+    packet = pl.pallas_call(
+        functools.partial(pack_kernel, copies, reach),
+        out_shape=jax.ShapeDtypeStruct((copies, PACKET, LANES), jnp.float32),
+        in_specs=[smem] + [vmem] * 5,
+        out_specs=vmem,
+        scratch_shapes=[pltpu.VMEM((SIDE, LANES), jnp.float32)],
+        name="pack",
+    )(owner.reshape(-1), estimate.reshape(SIDE, LANES), view_data.reshape(DATA_ROWS, LANES), taps_x, taps_y, taps_z)
+    alike = [[(2 * g + c) * blocks + b for g in range(groups) for b in range(blocks)] for c in range(2)]
+    near = lax.all_to_all(packet, ("view", "block"), 0, 0, axis_index_groups=alike, tiled=True)
+    near = near.reshape(copies * PACKET, LANES)
+    far = lax.ppermute(near, "view", [(v, v ^ 1) for v in range(views)])
+    joined = pl.pallas_call(
+        functools.partial(volume_kernel, blocks, groups, reach),
+        out_shape=jax.ShapeDtypeStruct((SIDE, LANES), jnp.float32),
+        in_specs=[vmem] * 2,
+        out_specs=vmem,
+        scratch_shapes=[pltpu.VMEM((SIDE * SIDE, LANES), jnp.float32)],
+        name="volume",
+    )(near, far)
+    return joined.reshape(estimate.shape)
+
+
+def fits_one_device(estimate, view_data, taps_x, blocks, views):
+    thin, total_y, depth = estimate.shape
+    reach = taps_x.shape[1] // 2
+    return (
+        (thin, blocks, total_y, depth) == (1, SIDE, SIDE, LANES)
+        and view_data.shape[1] == 2
+        and views == 4
+        and taps_x.shape[1] % 2 == 1
+        and reach < LANES // 2
+    )
 
 
 def band_matrix(taps, length):
@@ -24,6 +216,8 @@
 def on_device(estimate, view_data, taps_x, taps_y, taps_z, owner):
     blocks = lax.axis_size("block")
     views = lax.axis_size("view")
+    if fits_one_device(estimate, view_data, taps_x, blocks, views):
+        return on_device_small(estimate, view_data, taps_x, taps_y, taps_z, owner)
     thin = estimate.shape[0]
     total_y = estimate.shape[1]
     depth = estimate.shape[2]

time: 90.8 us -> 25.5 us (0.28)
  other arithmetic: 29.9 us -> 0 us
  starting transfers between devices: 13.4 us -> 0.01 us
  blocking collectives: 29.1 us -> 16.7 us
  local copies, waits for them, and re-layouts: 8.93 us -> 0.69 us
  Pallas kernels: 0 us -> 6.46 us
  waiting for transfers between devices: 6.51 us -> 1.44 us
  matrix products: 1.99 us -> 0 us
    select_n x4 -> x0, other arithmetic: 16.4 us -> none  [the longest x2 16.4 us: band_matrix(): return jnp.where(inside, values, jnp.zeros_like(values))]
    all_to_all x2 -> x0, starting transfers between devices: 13.4 us -> none  [the longest x1 7.42 us: on_device(): lax.all_to_all(picked, 'block', split_axis=1, concat_axis=1, tiled=True)]
    psum x2 -> x0, blocking collectives: 11.3 us -> none  [on_device(): logs = lax.psum(jnp.log(corr), 'view')]
    gather x5 -> x0, other arithmetic: 10.1 us -> none  [the longest x2 10 us: band_matrix(): values = jnp.take(taps, index.reshape(-1), axis=0).reshape(length, length)]
    all_to_all x2 -> x0, waiting for transfers between devices: 6.51 us -> none  [the longest x1 6.51 us: on_device(): lax.all_to_all(back.reshape(slots, blocks, thin, thin, depth), 'block', s...]
    pallas_call x0 -> x2, Pallas kernels: none -> 6.46 us  [the longest x1 4.91 us: on_device_small(): pl.pallas_call(functools.partial(volume_kernel, blocks, groups, reach), o...]
    gather x8 -> x0, local copies, waits for them, and re-layouts: 5.23 us -> none  [the longest x4 2.99 us: band_matrix(): values = jnp.take(taps, index.reshape(-1), axis=0).reshape(length, length)]
    dot_general x12 -> x0, matrix products: 1.99 us -> none  [the longest x2 0.39 us: on_device(): blurred = jnp.einsum('sxyj,ij->sxyi', blurred, m_z, precision=HIGH)]
  transfers between devices with their start and end apart: 2 -> 1, of which waited for: 1 -> 1; matrix products, arithmetic and copies ran while one was open for 33% -> 0% of each run, Pallas kernels for 0% -> 0%
where the time goes in v1:
time: 25.5 us; the launch traced here: 25.3 us
  blocking collectives  16.7 us (65%)
  Pallas kernels  6.46 us (25%)
  waiting for transfers between devices  1.44 us (6%)
  local copies, waits for them, and re-layouts  0.69 us (3%)
    all_to_all x1, blocking collectives, on_device_small(): lax.all_to_all(packet, ('view', 'block'), 0, 0, axis_index_groups=alike,...  16.7 us
    pallas_call x1, Pallas kernels, on_device_small(): pl.pallas_call(functools.partial(volume_kernel, blocks, groups, reach), o...  4.91 us
    pallas_call x1, Pallas kernels, on_device_small(): pl.pallas_call(functools.partial(pack_kernel, copies, reach), out_shape=j...  1.56 us
    ppermute x1, waiting for transfers between devices, on_device_small(): far = lax.ppermute(near, 'view', [(v, v ^ 1) for v in range(views)])  1.44 us
    unnamed x4, local copies, waits for them, and re-layouts  0.69 us
  transfers between devices with their start and end apart: 1, of which 1 were waited for; matrix products, arithmetic and copies ran while one was open for 0% of the time, Pallas kernels for 0%

profile of v1, /device:TPU:0, one launch (start us, length us, event | category | flops | bytes accessed | tf_op | source)
XLA Modules:
  0.0 25.3 jit_solution(15102046406337830237)
XLA Ops:
  0.0 1.6 %pack.1 = f32[16,24,128]{2,1,0:T(8,128)} custom-call(s32[8]{0:T(128)} %bitcast.9, f32[8,128]{1,0:T(8,128)} %bitcast.8, f32[16,128]{1,0:T(8,128)} %bitcast.7, f32[1,33]{1,0:T(1,128)} %tx.1, f32[1,33]{1,0:T(1,128)} %ty.1, f32[1,33]{1,0:T(1,128)} %tz.1), custom_call_target="tpu_custom_call" | custom-call | tf_op jit(solution)/shard_map/pack/pallas_call | solution.py:169
  1.6 16.7 %all_to_all.5 = f32[16,24,128]{2,1,0:T(8,128)S(1)} all-to-all(f32[16,24,128]{2,1,0:T(8,128)} %pack.1), channel_id=1, replica_groups={{0,1,2,3,4,5,6,7,16,17,18,19,20,21,22,23},{8,9,10,11,12,13,14,15,24,25,..., dimensions={0} | all-to-all | bytes 393216 | tf_op jit(solution)/shard_map/all_to_all | solution.py:178
  18.2 0.0 copy-start
  18.2 0.0 collective-permute-start
  18.3 1.4 %collective-permute-done.far = f32[384,128]{1,0:T(8,128)S(1)} collective-permute-done((f32[384,128]{1,0:T(8,128)S(1)}, f32[384,128]{1,0:T(8,128)S(1)}, u32[]{:S(2)}, u32[]{:S(2)}) %collective-permute-start) | collective-permute-done | bytes 196640 | tf_op jit(solution)/shard_map/ppermute | solution.py:180
  19.7 0.0 copy-done
  19.7 0.0 copy-start.1
  19.7 0.7 %copy-done.1 = f32[384,128]{1,0:T(8,128)} copy-done((f32[384,128]{1,0:T(8,128)}, f32[384,128]{1,0:T(8,128)S(1)}, u32[]{:S(2)}) %copy-start.1) | copy-done | bytes 196632
  20.4 4.9 %volume.1 = f32[8,128]{1,0:T(8,128)} custom-call(f32[384,128]{1,0:T(8,128)} %bitcast.6, f32[384,128]{1,0:T(8,128)} %copy-done.1), custom_call_target="tpu_custom_call" | custom-call | tf_op jit(solution)/shard_map/volume/pallas_call | solution.py:181
Async XLA Ops:
  18.2 1.4 %copy-start = (f32[16,24,128]{2,1,0:T(8,128)}, f32[16,24,128]{2,1,0:T(8,128)S(1)}, u32[]{:S(2)}) copy-start(f32[16,24,128]{2,1,0:T(8,128)S(1)} %all_to_all.5) | copy-start | bytes 589828
  18.2 1.4 %collective-permute-start = (f32[384,128]{1,0:T(8,128)S(1)}, f32[384,128]{1,0:T(8,128)S(1)}, u32[]{:S(2)}, u32[]{:S(2)}) collective-permute-start(f32[384,128]{1,0:T(8,128)S(1)} %bitcast.5), channel_id=1, source_target_pairs={{0,8},{8,0},{16,24},{24,16},{1,9},{9,1},{17,25},{25,17},{2,10},{10... | collective-permute-start | bytes 589832 | tf_op jit(solution)/shard_map/ppermute | solution.py:180
  19.7 0.7 %copy-start.1 = (f32[384,128]{1,0:T(8,128)}, f32[384,128]{1,0:T(8,128)S(1)}, u32[]{:S(2)}) copy-start(f32[384,128]{1,0:T(8,128)S(1)} %collective-permute-done.far) | copy-start | bytes 589828

commit v2 on v1

--- a/solution.py
+++ b/solution.py
@@ -168,7 +168,7 @@
     vmem = pl.BlockSpec(memory_space=pltpu.VMEM)
     packet = pl.pallas_call(
         functools.partial(pack_kernel, copies, reach),
-        out_shape=jax.ShapeDtypeStruct((copies, PACKET, LANES), jnp.float32),
+        out_shape=pltpu.VMEM((copies, PACKET, LANES), jnp.float32),
         in_specs=[smem] + [vmem] * 5,
         out_specs=vmem,
         scratch_shapes=[pltpu.VMEM((SIDE, LANES), jnp.float32)],
@@ -178,6 +178,8 @@
     near = lax.all_to_all(packet, ("view", "block"), 0, 0, axis_index_groups=alike, tiled=True)
     near = near.reshape(copies * PACKET, LANES)
     far = lax.ppermute(near, "view", [(v, v ^ 1) for v in range(views)])
+    near = pltpu.with_memory_space_constraint(near, pltpu.VMEM)
+    far = pltpu.with_memory_space_constraint(far, pltpu.VMEM)
     joined = pl.pallas_call(
         functools.partial(volume_kernel, blocks, groups, reach),
         out_shape=jax.ShapeDtypeStruct((SIDE, LANES), jnp.float32),

time: 25.5 us -> 22.9 us (0.90)
  Pallas kernels: 6.46 us -> 4.78 us
  local copies, waits for them, and re-layouts: 0.69 us -> 0 us
    pallas_call x1, Pallas kernels: 4.91 us -> 3.89 us  [on_device_small(): pl.pallas_call(functools.partial(volume_kernel, blocks, groups, reach), o...]
    unnamed x4 -> x0, local copies, waits for them, and re-layouts: 0.69 us -> none
    pallas_call x1, Pallas kernels: 1.56 us -> 0.89 us  [on_device_small(): pl.pallas_call(functools.partial(pack_kernel, copies, reach), out_shape=p...]
where the time goes in v2:
time: 22.9 us; the launch traced here: 22.7 us
  blocking collectives  16.5 us (72%)
  Pallas kernels  4.78 us (21%)
  waiting for transfers between devices  1.44 us (6%)
    all_to_all x1, blocking collectives, on_device_small(): lax.all_to_all(packet, ('view', 'block'), 0, 0, axis_index_groups=alike,...  16.5 us
    pallas_call x1, Pallas kernels, on_device_small(): pl.pallas_call(functools.partial(volume_kernel, blocks, groups, reach), o...  3.89 us
    ppermute x1, waiting for transfers between devices, on_device_small(): far = lax.ppermute(near, 'view', [(v, v ^ 1) for v in range(views)])  1.44 us
    pallas_call x1, Pallas kernels, on_device_small(): pl.pallas_call(functools.partial(pack_kernel, copies, reach), out_shape=p...  0.89 us
  transfers between devices with their start and end apart: 1, of which 1 were waited for; matrix products, arithmetic and copies ran while one was open for 0% of the time, Pallas kernels for 0%

profile of v2, /device:TPU:0, one launch (start us, length us, event | category | flops | bytes accessed | tf_op | source)
XLA Modules:
  0.0 22.7 jit_solution(4888040370329639420)
XLA Ops:
  0.0 0.9 %pack.1 = f32[16,24,128]{2,1,0:T(8,128)S(1)} custom-call(s32[8]{0:T(128)} %bitcast.9, f32[8,128]{1,0:T(8,128)} %bitcast.8, f32[16,128]{1,0:T(8,128)} %bitcast.7, f32[1,33]{1,0:T(1,128)} %tx.1, f32[1,33]{1,0:T(1,128)} %ty.1, f32[1,33]{1,0:T(1,128)} %tz.1), custom_call_target="tpu_custom_call" | custom-call | tf_op jit(solution)/shard_map/pack/pallas_call | solution.py:169
  0.9 16.5 %all_to_all.5 = f32[16,24,128]{2,1,0:T(8,128)S(1)} all-to-all(f32[16,24,128]{2,1,0:T(8,128)S(1)} %pack.1), channel_id=1, replica_groups={{0,1,2,3,4,5,6,7,16,17,18,19,20,21,22,23},{8,9,10,11,12,13,14,15,24,25,..., dimensions={0} | all-to-all | bytes 393216 | tf_op jit(solution)/shard_map/all_to_all | solution.py:178
  17.4 0.0 collective-permute-start
  17.4 1.4 %collective-permute-done.far = f32[384,128]{1,0:T(8,128)S(1)} collective-permute-done((f32[384,128]{1,0:T(8,128)S(1)}, f32[384,128]{1,0:T(8,128)S(1)}, u32[]{:S(2)}, u32[]{:S(2)}) %collective-permute-start) | collective-permute-done | bytes 196640 | tf_op jit(solution)/shard_map/ppermute | solution.py:180
  18.8 3.9 %volume.1 = f32[8,128]{1,0:T(8,128)} custom-call(f32[384,128]{1,0:T(8,128)S(1)} %bitcast.6, f32[384,128]{1,0:T(8,128)S(1)} %collective-permute-done.far), custom_call_target="tpu_custom_call" | custom-call | tf_op jit(solution)/shard_map/volume/pallas_call | solution.py:183
Async XLA Ops:
  17.4 1.4 %collective-permute-start = (f32[384,128]{1,0:T(8,128)S(1)}, f32[384,128]{1,0:T(8,128)S(1)}, u32[]{:S(2)}, u32[]{:S(2)}) collective-permute-start(f32[384,128]{1,0:T(8,128)S(1)} %bitcast.5), channel_id=1, source_target_pairs={{0,8},{8,0},{16,24},{24,16},{1,9},{9,1},{17,25},{25,17},{2,10},{10... | collective-permute-start | bytes 589832 | tf_op jit(solution)/shard_map/ppermute | solution.py:180

commit v3 on v2

--- a/solution.py
+++ b/solution.py
@@ -25,34 +25,24 @@
     return lax.broadcasted_iota(jnp.int32, (rows, LANES), 0)
 
 
-def pack_kernel(copies, reach, own, est, data, tx, ty, tz, out, taps):
+def pack_kernel(copies, own, est, data, tx, ty, tz, out, meta):
     block = lax.axis_index("block")
     view = lax.axis_index("view")
-    width = 2 * reach + 1
-    taps[...] = jnp.zeros_like(taps)
-    taps[2:3, :width] = tz[...]
-    taps[3:4, :width] = tx[...]
-    taps[4:5, :width] = tx[...]
-    taps[5:6, :width] = ty[...]
+    width = tx.shape[1]
     first = jnp.int32(-1)
     second = jnp.int32(-1)
     for y in range(SIDE):
         mine = own[y] == block
         second = jnp.where(mine & (first >= 0), y, second)
         first = jnp.where(mine & (first < 0), y, first)
-    lane = lane_ids(SIDE)
+    lane = lane_ids(1)
+    meta[...] = jnp.where(lane == 3 * width, first, second).astype(jnp.float32)
+    for k, taps in enumerate((tx, ty, tz)):
+        meta[:, k * width : (k + 1) * width] = taps[...]
     row = row_ids(SIDE)
-    along_z = jnp.where(lane < LANES // 2, lane, lane - LANES) + reach
-    along_x = (lane & (SIDE - 1)) + reach
-    along_y = (lane >> 3) + jnp.where(lane < LANES // 2, reach, reach - 16)
-    index = jnp.where(row == 2, along_z, jnp.where(row == 3, along_x, jnp.where(row == 4, along_x - SIDE, along_y)))
-    inside = (index >= 0) & (index < width)
-    picked = jnp.take_along_axis(taps[...], jnp.clip(index, 0, width - 1), axis=1)
-    tile = jnp.where(inside, picked, 0.0)
+    tile = jnp.broadcast_to(meta[...], (SIDE, LANES))
     for k in range(2):
         tile = jnp.where(row == k, est[pl.ds(2 * view + k, 1), :], tile)
-    tile = jnp.where(row == 6, first.astype(jnp.float32), tile)
-    tile = jnp.where(row == 7, second.astype(jnp.float32), tile)
     lower, upper = data[:SIDE], data[SIDE:]
     for k in range(copies):
         out[k, :SIDE] = lower
@@ -70,42 +60,26 @@
     return jnp.dot(a, b, preferred_element_type=jnp.float32)
 
 
-def per_side(matrix):
-    doubled = jnp.concatenate([matrix, matrix], axis=1)
-    high, low = halves(doubled)
-    both = jnp.where(lane_ids(matrix.shape[0]) < matrix.shape[1], high.astype(jnp.float32), low.astype(jnp.float32))
-    both = both.astype(jnp.bfloat16)
-    return jnp.concatenate([both, both], axis=1)
-
-
-def per_depth(matrix):
-    high, low = halves(matrix)
-    row = jnp.concatenate([high, low], axis=1)
-    return jnp.concatenate([row, row], axis=0)
-
-
-def apply_side(sided, value):
+def left(value):
     high, low = halves(value)
-    return matmul(sided, jnp.concatenate([high, high, low, low], axis=0))
-
-
-def apply_depth(value, deep):
+    return jnp.concatenate([high, low, high], axis=1)
+
+
+def right(value):
     high, low = halves(value)
-    both = matmul(jnp.concatenate([high, low], axis=1), deep)
-    return both[:, :LANES] + both[:, LANES:]
-
-
-def geometric_mean(values):
-    if len(values) == 1:
-        return values[0]
-    half = len(values) // 2
-    return jnp.sqrt(geometric_mean(values[:half]) * geometric_mean(values[half:]))
+    return jnp.concatenate([high, high, low], axis=0)
+
+
+def lane_pick(tile, index):
+    return jnp.take_along_axis(tile, index, axis=1)
 
 
 def volume_kernel(blocks, groups, reach, near, far, out, held):
     block = lax.axis_index("block")
     core = lax.axis_index("view") & 1
+    width = 2 * reach + 1
     sources = [(ref, g * blocks * PACKET) for ref in (near, far) for g in range(groups)]
+    views = range(len(sources))
 
     tiles = []
     for y in range(SIDE):
@@ -117,43 +91,59 @@
     est = jnp.concatenate(tiles, axis=0)
 
     lane, row = lane_ids(SIDE), row_ids(SIDE)
+    lane_x, lane_y = lane & (SIDE - 1), lane >> 3
+    signed = jnp.where(lane < LANES // 2, lane, lane - LANES)
+
+    def kernel_row(meta, which, offset):
+        inside = (offset >= -reach) & (offset <= reach)
+        index = jnp.clip(offset, -reach, reach) + (which * width + reach)
+        return jnp.where(inside, lane_pick(meta, index), 0.0)
+
     band = jnp.abs(lane_ids(LANES) - row_ids(LANES)) <= reach
-    recorded, forward_side, forward_depth, back_side, back_depth = [], [], [], [], []
+
+    def toeplitz(base):
+        rolled = pltpu.roll(jnp.tile(base, (LANES // SIDE, 1)), 0, 1, stride=1, stride_axis=0)
+        return jnp.where(band, rolled, 0.0)
+
+    forward_side, forward_depth, back_side, back_depth = [], [], [], []
+    metas = []
     for ref, start in sources:
+        at = start + DATA_ROWS + 2
+        meta = jnp.broadcast_to(ref[at : at + 1, :], (SIDE, LANES))
+        metas.append(meta)
+        forward_depth.append(right(toeplitz(kernel_row(meta, 2, -signed))))
+    forward_depth = jnp.concatenate(forward_depth, axis=1)
+    for meta in metas:
+        for sign, sides in ((1, forward_side), (-1, back_side)):
+            x_tile = kernel_row(meta, 0, sign * (lane_x - row))
+            y_tile = kernel_row(meta, 1, sign * (lane_y - row))
+            side = jnp.concatenate([x_tile * y_tile[y : y + 1, :] for y in range(SIDE)], axis=0)
+            sides.append(left(side[:, : SIDE * SIDE]))
+    recorded = []
+    for ref, start in sources:
+        labels = ref[pl.ds(start + DATA_ROWS + 2, blocks, stride=PACKET), :]
         slabs = [jnp.zeros((SIDE, LANES), jnp.float32)] * SIDE
-        for b in range(blocks):
-            at = start + b * PACKET
-            for s in range(2):
-                label = jnp.broadcast_to(ref[at + DATA_ROWS + 6 + s : at + DATA_ROWS + 7 + s, :], (SIDE, LANES))
-                slab = ref[at + s * SIDE : at + (s + 1) * SIDE, :]
+        for s in range(2):
+            spread = lane_pick(labels, jnp.full((SIDE, LANES), 3 * width + s, jnp.int32))
+            for b in range(blocks):
+                at = start + b * PACKET + s * SIDE
+                label = jnp.broadcast_to(spread[b : b + 1, :], (SIDE, LANES))
+                slab = ref[at : at + SIDE, :]
                 for y in range(SIDE):
                     slabs[y] = jnp.where(label == y, slab, slabs[y])
         recorded.append(jnp.concatenate(slabs, axis=0))
-
-        def meta(k, rows):
-            at = start + DATA_ROWS + k
-            return jnp.broadcast_to(ref[at : at + 1, :], (rows, LANES))
-
-        deep = pltpu.roll(meta(2, LANES), 0, 1, stride=1, stride_axis=0)
-        deep = jnp.where(band, deep, 0.0)
-        forward_depth.append(per_depth(deep.T))
-        back_depth.append(per_depth(deep))
-        upper = pltpu.roll(meta(3, SIDE), 0, 1, stride=1, stride_axis=0)
-        lower = pltpu.roll(meta(4, SIDE), 0, 1, stride=1, stride_axis=0)
-        x_tile = jnp.where((lane & (SIDE - 1)) >= row, upper, lower)
-        y_tile = pltpu.roll(meta(5, SIDE), 0, 1, stride=SIDE, stride_axis=0)
-        side = jnp.concatenate([x_tile * y_tile[y : y + 1, :] for y in range(SIDE)], axis=0)
-        side = side[:, : SIDE * SIDE]
-        forward_side.append(per_side(side))
-        back_side.append(per_side(side.T))
+    for meta in metas:
+        back_depth.append(right(toeplitz(kernel_row(meta, 2, signed))))
 
     for step in range(ITERS):
-        corrections = []
-        for v in range(len(sources)):
-            blurred = apply_side(forward_side[v], apply_depth(est, forward_depth[v]))
-            ratio = recorded[v] / blurred
-            corrections.append(apply_depth(apply_side(back_side[v], ratio), back_depth[v]))
-        est = est * geometric_mean(corrections)
+        deep = matmul(left(est), forward_depth)
+        deep = [right(deep[:, v * LANES : (v + 1) * LANES]) for v in views]
+        blurred = [matmul(forward_side[v], deep[v]) for v in views]
+        ratios = [right(recorded[v] / blurred[v]) for v in views]
+        spread = [left(matmul(back_side[v], ratios[v])) for v in views]
+        corr = [matmul(spread[v], back_depth[v]) for v in views]
+        roots = [lax.rsqrt(corr[v] * corr[v + 1]) for v in views[::2]]
+        est = est * lax.rsqrt(roots[0] * roots[1])
     held[...] = est
     out[...] = held[pl.ds(block, SIDE, stride=SIDE), :]
 
@@ -167,11 +157,11 @@
     smem = pl.BlockSpec(memory_space=pltpu.SMEM)
     vmem = pl.BlockSpec(memory_space=pltpu.VMEM)
     packet = pl.pallas_call(
-        functools.partial(pack_kernel, copies, reach),
+        functools.partial(pack_kernel, copies),
         out_shape=pltpu.VMEM((copies, PACKET, LANES), jnp.float32),
         in_specs=[smem] + [vmem] * 5,
         out_specs=vmem,
-        scratch_shapes=[pltpu.VMEM((SIDE, LANES), jnp.float32)],
+        scratch_shapes=[pltpu.VMEM((1, LANES), jnp.float32)],
         name="pack",
     )(owner.reshape(-1), estimate.reshape(SIDE, LANES), view_data.reshape(DATA_ROWS, LANES), taps_x, taps_y, taps_z)
     alike = [[(2 * g + c) * blocks + b for g in range(groups) for b in range(blocks)] for c in range(2)]
@@ -193,13 +183,12 @@
 
 def fits_one_device(estimate, view_data, taps_x, blocks, views):
     thin, total_y, depth = estimate.shape
-    reach = taps_x.shape[1] // 2
     return (
         (thin, blocks, total_y, depth) == (1, SIDE, SIDE, LANES)
         and view_data.shape[1] == 2
         and views == 4
         and taps_x.shape[1] % 2 == 1
-        and reach < LANES // 2
+        and 3 * taps_x.shape[1] + 2 <= LANES
     )
 
 

time: 22.9 us -> 21.2 us (0.926)
  Pallas kernels: 4.78 us -> 3.08 us
    pallas_call x1, Pallas kernels: 3.89 us -> 2.2 us  [on_device_small(): pl.pallas_call(functools.partial(volume_kernel, blocks, groups, reach), o...]
where the time goes in v3:
time: 21.2 us; the launch traced here: 21 us
  blocking collectives  16.5 us (78%)
  Pallas kernels  3.08 us (15%)
  waiting for transfers between devices  1.44 us (7%)
    all_to_all x1, blocking collectives, on_device_small(): lax.all_to_all(packet, ('view', 'block'), 0, 0, axis_index_groups=alike,...  16.5 us
    pallas_call x1, Pallas kernels, on_device_small(): pl.pallas_call(functools.partial(volume_kernel, blocks, groups, reach), o...  2.2 us
    ppermute x1, waiting for transfers between devices, on_device_small(): far = lax.ppermute(near, 'view', [(v, v ^ 1) for v in range(views)])  1.44 us
    pallas_call x1, Pallas kernels, on_device_small(): pl.pallas_call(functools.partial(pack_kernel, copies), out_shape=pltpu.VM...  0.88 us
  transfers between devices with their start and end apart: 1, of which 1 were waited for; matrix products, arithmetic and copies ran while one was open for 0% of the time, Pallas kernels for 0%

profile of v3, /device:TPU:0, one launch (start us, length us, event | category | flops | bytes accessed | tf_op | source)
XLA Modules:
  0.0 21.0 jit_solution(15093019232373659284)
XLA Ops:
  0.0 0.9 %pack.1 = f32[16,24,128]{2,1,0:T(8,128)S(1)} custom-call(s32[8]{0:T(128)} %bitcast.9, f32[8,128]{1,0:T(8,128)} %bitcast.8, f32[16,128]{1,0:T(8,128)} %bitcast.7, f32[1,33]{1,0:T(1,128)} %tx.1, f32[1,33]{1,0:T(1,128)} %ty.1, f32[1,33]{1,0:T(1,128)} %tz.1), custom_call_target="tpu_custom_call" | custom-call | tf_op jit(solution)/shard_map/pack/pallas_call | solution.py:159
  0.9 16.5 %all_to_all.5 = f32[16,24,128]{2,1,0:T(8,128)S(1)} all-to-all(f32[16,24,128]{2,1,0:T(8,128)S(1)} %pack.1), channel_id=1, replica_groups={{0,1,2,3,4,5,6,7,16,17,18,19,20,21,22,23},{8,9,10,11,12,13,14,15,24,25,..., dimensions={0} | all-to-all | bytes 393216 | tf_op jit(solution)/shard_map/all_to_all | solution.py:168
  17.4 0.0 collective-permute-start
  17.4 1.4 %collective-permute-done.far = f32[384,128]{1,0:T(8,128)S(1)} collective-permute-done((f32[384,128]{1,0:T(8,128)S(1)}, f32[384,128]{1,0:T(8,128)S(1)}, u32[]{:S(2)}, u32[]{:S(2)}) %collective-permute-start) | collective-permute-done | bytes 196640 | tf_op jit(solution)/shard_map/ppermute | solution.py:170
  18.8 2.2 %volume.1 = f32[8,128]{1,0:T(8,128)} custom-call(f32[384,128]{1,0:T(8,128)S(1)} %bitcast.6, f32[384,128]{1,0:T(8,128)S(1)} %collective-permute-done.far), custom_call_target="tpu_custom_call" | custom-call | tf_op jit(solution)/shard_map/volume/pallas_call | solution.py:173
Async XLA Ops:
  17.4 1.4 %collective-permute-start = (f32[384,128]{1,0:T(8,128)S(1)}, f32[384,128]{1,0:T(8,128)S(1)}, u32[]{:S(2)}, u32[]{:S(2)}) collective-permute-start(f32[384,128]{1,0:T(8,128)S(1)} %bitcast.5), channel_id=1, source_target_pairs={{0,8},{8,0},{16,24},{24,16},{1,9},{9,1},{17,25},{25,17},{2,10},{10... | collective-permute-start | bytes 589832 | tf_op jit(solution)/shard_map/ppermute | solution.py:170

commit v4 on v3

--- a/solution.py
+++ b/solution.py
@@ -15,6 +15,7 @@
 LANES = 128
 DATA_ROWS = 16
 PACKET = 24
+FIRST = 5
 
 
 def lane_ids(rows):
@@ -84,7 +85,7 @@
     tiles = []
     for y in range(SIDE):
         view, k = y // 2, y % 2
-        start = (view // 2) * blocks * PACKET + DATA_ROWS + k
+        start = (groups - 1 - view // 2) * blocks * PACKET + DATA_ROWS + k
         rows = pl.ds(start, blocks, stride=PACKET)
         same = (core == view % 2).astype(jnp.int32) > 0
         tiles.append(jnp.where(same, near[rows, :], far[rows, :]))
@@ -92,6 +93,7 @@
 
     lane, row = lane_ids(SIDE), row_ids(SIDE)
     lane_x, lane_y = lane & (SIDE - 1), lane >> 3
+    turned = lambda j: (j + FIRST) & (SIDE - 1)
     signed = jnp.where(lane < LANES // 2, lane, lane - LANES)
 
     def kernel_row(meta, which, offset):
@@ -114,9 +116,11 @@
         forward_depth.append(right(toeplitz(kernel_row(meta, 2, -signed))))
     forward_depth = jnp.concatenate(forward_depth, axis=1)
     for meta in metas:
-        for sign, sides in ((1, forward_side), (-1, back_side)):
-            x_tile = kernel_row(meta, 0, sign * (lane_x - row))
-            y_tile = kernel_row(meta, 1, sign * (lane_y - row))
+        forward = (turned(lane_x) - row, lane_y - row, forward_side)
+        back = (turned(row) - lane_x, row - lane_y, back_side)
+        for x_offset, y_offset, sides in (forward, back):
+            x_tile = kernel_row(meta, 0, x_offset)
+            y_tile = kernel_row(meta, 1, y_offset)
             side = jnp.concatenate([x_tile * y_tile[y : y + 1, :] for y in range(SIDE)], axis=0)
             sides.append(left(side[:, : SIDE * SIDE]))
     recorded = []
@@ -145,7 +149,7 @@
         roots = [lax.rsqrt(corr[v] * corr[v + 1]) for v in views[::2]]
         est = est * lax.rsqrt(roots[0] * roots[1])
     held[...] = est
-    out[...] = held[pl.ds(block, SIDE, stride=SIDE), :]
+    out[...] = held[pl.ds((block - FIRST) & (SIDE - 1), SIDE, stride=SIDE), :]
 
 
 def on_device_small(estimate, view_data, taps_x, taps_y, taps_z, owner):
@@ -164,7 +168,8 @@
         scratch_shapes=[pltpu.VMEM((1, LANES), jnp.float32)],
         name="pack",
     )(owner.reshape(-1), estimate.reshape(SIDE, LANES), view_data.reshape(DATA_ROWS, LANES), taps_x, taps_y, taps_z)
-    alike = [[(2 * g + c) * blocks + b for g in range(groups) for b in range(blocks)] for c in range(2)]
+    ring = [(FIRST + j) % blocks for j in range(blocks)]
+    alike = [[(2 * g + c) * blocks + b for g in reversed(range(groups)) for b in ring] for c in range(2)]
     near = lax.all_to_all(packet, ("view", "block"), 0, 0, axis_index_groups=alike, tiled=True)
     near = near.reshape(copies * PACKET, LANES)
     far = lax.ppermute(near, "view", [(v, v ^ 1) for v in range(views)])

time: 21.2 us -> 18.3 us (0.86)
  blocking collectives: 16.5 us -> 13.6 us
    all_to_all x1, blocking collectives: 16.5 us -> 13.6 us  [on_device_small(): lax.all_to_all(packet, ('view', 'block'), 0, 0, axis_index_groups=alike,...]
where the time goes in v4:
time: 18.3 us; the launch traced here: 18.1 us
  blocking collectives  13.6 us (74%)
  Pallas kernels  3.09 us (17%)
  waiting for transfers between devices  1.44 us (8%)
    all_to_all x1, blocking collectives, on_device_small(): lax.all_to_all(packet, ('view', 'block'), 0, 0, axis_index_groups=alike,...  13.6 us
    pallas_call x1, Pallas kernels, on_device_small(): pl.pallas_call(functools.partial(volume_kernel, blocks, groups, reach), o...  2.2 us
    ppermute x1, waiting for transfers between devices, on_device_small(): far = lax.ppermute(near, 'view', [(v, v ^ 1) for v in range(views)])  1.44 us
    pallas_call x1, Pallas kernels, on_device_small(): pl.pallas_call(functools.partial(pack_kernel, copies), out_shape=pltpu.VM...  0.88 us
  transfers between devices with their start and end apart: 1, of which 1 were waited for; matrix products, arithmetic and copies ran while one was open for 0% of the time, Pallas kernels for 0%

profile of v4, /device:TPU:0, one launch (start us, length us, event | category | flops | bytes accessed | tf_op | source)
XLA Modules:
  0.0 18.1 jit_solution(5180050884517430467)
XLA Ops:
  0.0 0.9 %pack.1 = f32[16,24,128]{2,1,0:T(8,128)S(1)} custom-call(s32[8]{0:T(128)} %bitcast.9, f32[8,128]{1,0:T(8,128)} %bitcast.8, f32[16,128]{1,0:T(8,128)} %bitcast.7, f32[1,33]{1,0:T(1,128)} %tx.1, f32[1,33]{1,0:T(1,128)} %ty.1, f32[1,33]{1,0:T(1,128)} %tz.1), custom_call_target="tpu_custom_call" | custom-call | tf_op jit(solution)/shard_map/pack/pallas_call | solution.py:163
  0.9 13.6 %all_to_all.5 = f32[16,24,128]{2,1,0:T(8,128)S(1)} all-to-all(f32[16,24,128]{2,1,0:T(8,128)S(1)} %pack.1), channel_id=1, replica_groups={{21,22,23,16,17,18,19,20,5,6,7,0,1,2,3,4},{29,30,31,24,25,26,27,28,13,1..., dimensions={0} | all-to-all | bytes 393216 | tf_op jit(solution)/shard_map/all_to_all | solution.py:173
  14.5 0.0 collective-permute-start
  14.5 1.4 %collective-permute-done.far = f32[384,128]{1,0:T(8,128)S(1)} collective-permute-done((f32[384,128]{1,0:T(8,128)S(1)}, f32[384,128]{1,0:T(8,128)S(1)}, u32[]{:S(2)}, u32[]{:S(2)}) %collective-permute-start) | collective-permute-done | bytes 196640 | tf_op jit(solution)/shard_map/ppermute | solution.py:175
  15.9 2.2 %volume.1 = f32[8,128]{1,0:T(8,128)} custom-call(f32[384,128]{1,0:T(8,128)S(1)} %bitcast.6, f32[384,128]{1,0:T(8,128)S(1)} %collective-permute-done.far), custom_call_target="tpu_custom_call" | custom-call | tf_op jit(solution)/shard_map/volume/pallas_call | solution.py:178
Async XLA Ops:
  14.5 1.4 %collective-permute-start = (f32[384,128]{1,0:T(8,128)S(1)}, f32[384,128]{1,0:T(8,128)S(1)}, u32[]{:S(2)}, u32[]{:S(2)}) collective-permute-start(f32[384,128]{1,0:T(8,128)S(1)} %bitcast.5), channel_id=1, source_target_pairs={{0,8},{8,0},{16,24},{24,16},{1,9},{9,1},{17,25},{25,17},{2,10},{10... | collective-permute-start | bytes 589832 | tf_op jit(solution)/shard_map/ppermute | solution.py:175

commit v5 on v4

--- a/solution.py
+++ b/solution.py
@@ -14,8 +14,18 @@
 SIDE = 8
 LANES = 128
 DATA_ROWS = 16
-PACKET = 24
+EST_ROWS = 4
+META = DATA_ROWS + EST_ROWS
+PACKET = META + 1
 FIRST = 5
+
+
+def turned(j):
+    return (j + FIRST) & (SIDE - 1)
+
+
+def late(j):
+    return int(turned(j) >= SIDE // 2)
 
 
 def lane_ids(rows):
@@ -28,7 +38,7 @@
 
 def pack_kernel(copies, own, est, data, tx, ty, tz, out, meta):
     block = lax.axis_index("block")
-    view = lax.axis_index("view")
+    group = lax.axis_index("view") >> 1
     width = tx.shape[1]
     first = jnp.int32(-1)
     second = jnp.int32(-1)
@@ -36,19 +46,18 @@
         mine = own[y] == block
         second = jnp.where(mine & (first >= 0), y, second)
         first = jnp.where(mine & (first < 0), y, first)
-    lane = lane_ids(1)
-    meta[...] = jnp.where(lane == 3 * width, first, second).astype(jnp.float32)
+    meta[...] = jnp.where(lane_ids(1) == 3 * width, first, second).astype(jnp.float32)
     for k, taps in enumerate((tx, ty, tz)):
         meta[:, k * width : (k + 1) * width] = taps[...]
-    row = row_ids(SIDE)
-    tile = jnp.broadcast_to(meta[...], (SIDE, LANES))
-    for k in range(2):
-        tile = jnp.where(row == k, est[pl.ds(2 * view + k, 1), :], tile)
+    row = meta[...]
+    share = jnp.where(group == 0, est[:EST_ROWS, :], est[EST_ROWS:, :])
     lower, upper = data[:SIDE], data[SIDE:]
     for k in range(copies):
-        out[k, :SIDE] = lower
-        out[k, SIDE:DATA_ROWS] = upper
-        out[k, DATA_ROWS:] = tile
+        at = k * PACKET
+        out[at : at + SIDE, :] = lower
+        out[at + SIDE : at + DATA_ROWS, :] = upper
+        out[at + DATA_ROWS : at + META, :] = share
+        out[at + META : at + PACKET, :] = row
 
 
 def halves(value):
@@ -75,25 +84,39 @@
     return jnp.take_along_axis(tile, index, axis=1)
 
 
-def volume_kernel(blocks, groups, reach, near, far, out, held):
-    block = lax.axis_index("block")
-    core = lax.axis_index("view") & 1
+def placed(slabs, ref, groups, width, flip):
+    for g in range(groups):
+        start = g * SIDE * PACKET
+        labels = ref[pl.ds(start + META, SIDE, stride=PACKET), :]
+        for s in range(2):
+            spread = lane_pick(labels, jnp.full((SIDE, LANES), 3 * width + s, jnp.int32))
+            for j in range(SIDE):
+                at = start + j * PACKET + s * SIDE
+                label = jnp.broadcast_to(spread[j : j + 1, :], (SIDE, LANES))
+                slab = ref[at : at + SIDE, :]
+                mine = slabs[(late(j) ^ flip) * groups + g]
+                for y in range(SIDE):
+                    mine[y] = jnp.where(label == y, slab, mine[y])
+
+
+def blur(est, forward_depth, forward_side, views):
+    deep = matmul(left(est), forward_depth)
+    deep = [right(deep[:, v * LANES : (v + 1) * LANES]) for v in views]
+    return [matmul(forward_side[v], deep[v]) for v in views]
+
+
+def prepare_kernel(groups, reach, near, est_out, inverse, slabs_out, forward_depth, forward_side, back_side, back_depth):
     width = 2 * reach + 1
-    sources = [(ref, g * blocks * PACKET) for ref in (near, far) for g in range(groups)]
-    views = range(len(sources))
-
+    views = range(2 * groups)
     tiles = []
     for y in range(SIDE):
-        view, k = y // 2, y % 2
-        start = (groups - 1 - view // 2) * blocks * PACKET + DATA_ROWS + k
-        rows = pl.ds(start, blocks, stride=PACKET)
-        same = (core == view % 2).astype(jnp.int32) > 0
-        tiles.append(jnp.where(same, near[rows, :], far[rows, :]))
+        start = (groups - 1 - y // EST_ROWS) * SIDE * PACKET + DATA_ROWS + y % EST_ROWS
+        tiles.append(near[pl.ds(start, SIDE, stride=PACKET), :])
     est = jnp.concatenate(tiles, axis=0)
+    est_out[...] = est
 
     lane, row = lane_ids(SIDE), row_ids(SIDE)
     lane_x, lane_y = lane & (SIDE - 1), lane >> 3
-    turned = lambda j: (j + FIRST) & (SIDE - 1)
     signed = jnp.where(lane < LANES // 2, lane, lane - LANES)
 
     def kernel_row(meta, which, offset):
@@ -107,82 +130,111 @@
         rolled = pltpu.roll(jnp.tile(base, (LANES // SIDE, 1)), 0, 1, stride=1, stride_axis=0)
         return jnp.where(band, rolled, 0.0)
 
-    forward_side, forward_depth, back_side, back_depth = [], [], [], []
     metas = []
-    for ref, start in sources:
-        at = start + DATA_ROWS + 2
-        meta = jnp.broadcast_to(ref[at : at + 1, :], (SIDE, LANES))
-        metas.append(meta)
-        forward_depth.append(right(toeplitz(kernel_row(meta, 2, -signed))))
-    forward_depth = jnp.concatenate(forward_depth, axis=1)
-    for meta in metas:
-        forward = (turned(lane_x) - row, lane_y - row, forward_side)
-        back = (turned(row) - lane_x, row - lane_y, back_side)
-        for x_offset, y_offset, sides in (forward, back):
+    for v in views:
+        j = [late(j) for j in range(SIDE)].index(v // groups)
+        at = ((v % groups) * SIDE + j) * PACKET + META
+        metas.append(jnp.broadcast_to(near[at : at + 1, :], (SIDE, LANES)))
+    forward = [right(toeplitz(kernel_row(meta, 2, -signed))) for meta in metas]
+    sides = []
+    for v, meta in enumerate(metas):
+        for x_offset, y_offset, out in (
+            (turned(lane_x) - row, lane_y - row, forward_side),
+            (turned(row) - lane_x, row - lane_y, back_side),
+        ):
             x_tile = kernel_row(meta, 0, x_offset)
             y_tile = kernel_row(meta, 1, y_offset)
             side = jnp.concatenate([x_tile * y_tile[y : y + 1, :] for y in range(SIDE)], axis=0)
-            sides.append(left(side[:, : SIDE * SIDE]))
-    recorded = []
-    for ref, start in sources:
-        labels = ref[pl.ds(start + DATA_ROWS + 2, blocks, stride=PACKET), :]
-        slabs = [jnp.zeros((SIDE, LANES), jnp.float32)] * SIDE
-        for s in range(2):
-            spread = lane_pick(labels, jnp.full((SIDE, LANES), 3 * width + s, jnp.int32))
-            for b in range(blocks):
-                at = start + b * PACKET + s * SIDE
-                label = jnp.broadcast_to(spread[b : b + 1, :], (SIDE, LANES))
-                slab = ref[at : at + SIDE, :]
-                for y in range(SIDE):
-                    slabs[y] = jnp.where(label == y, slab, slabs[y])
-        recorded.append(jnp.concatenate(slabs, axis=0))
-    for meta in metas:
-        back_depth.append(right(toeplitz(kernel_row(meta, 2, signed))))
-
+            side = left(side[:, : SIDE * SIDE])
+            out[v] = side
+            if out is forward_side:
+                sides.append(side)
+    forward = jnp.concatenate(forward, axis=1)
+    forward_depth[...] = forward
+    blurred = blur(est, forward, sides, views)
+    slabs = [[jnp.zeros((SIDE, LANES), jnp.float32)] * SIDE for _ in views]
+    placed(slabs, near, groups, width, 0)
+    for v, meta in enumerate(metas):
+        back_depth[:, v * LANES : (v + 1) * LANES] = right(toeplitz(kernel_row(meta, 2, signed)))
+        slabs_out[v] = jnp.concatenate(slabs[v], axis=0)
+        inverse[v] = 1.0 / blurred[v]
+
+
+def finish_kernel(groups, width, far, est_in, inverse, slabs_in, forward_depth, forward_side, back_side, back_depth, out, held):
+    block = lax.axis_index("block")
+    views = range(2 * groups)
+    slabs = [[slabs_in[v, y * SIDE : (y + 1) * SIDE, :] for y in range(SIDE)] for v in views]
+    placed(slabs, far, groups, width, 1)
+    recorded = [jnp.concatenate(slabs[v], axis=0) for v in views]
+    est = est_in[...]
     for step in range(ITERS):
-        deep = matmul(left(est), forward_depth)
-        deep = [right(deep[:, v * LANES : (v + 1) * LANES]) for v in views]
-        blurred = [matmul(forward_side[v], deep[v]) for v in views]
-        ratios = [right(recorded[v] / blurred[v]) for v in views]
+        if step == 0:
+            ratios = [recorded[v] * inverse[v] for v in views]
+        else:
+            blurred = blur(est, forward_depth[...], [forward_side[v] for v in views], views)
+            ratios = [recorded[v] / blurred[v] for v in views]
+        ratios = [right(ratios[v]) for v in views]
         spread = [left(matmul(back_side[v], ratios[v])) for v in views]
-        corr = [matmul(spread[v], back_depth[v]) for v in views]
+        corr = [matmul(spread[v], back_depth[:, v * LANES : (v + 1) * LANES]) for v in views]
         roots = [lax.rsqrt(corr[v] * corr[v + 1]) for v in views[::2]]
         est = est * lax.rsqrt(roots[0] * roots[1])
     held[...] = est
     out[...] = held[pl.ds((block - FIRST) & (SIDE - 1), SIDE, stride=SIDE), :]
 
 
+def in_vmem(value):
+    return pltpu.with_memory_space_constraint(value, pltpu.VMEM)
+
+
 def on_device_small(estimate, view_data, taps_x, taps_y, taps_z, owner):
     blocks = lax.axis_size("block")
     views = lax.axis_size("view")
-    reach = taps_x.shape[1] // 2
+    width = taps_x.shape[1]
     groups = views // 2
     copies = groups * blocks
     smem = pl.BlockSpec(memory_space=pltpu.SMEM)
     vmem = pl.BlockSpec(memory_space=pltpu.VMEM)
     packet = pl.pallas_call(
         functools.partial(pack_kernel, copies),
-        out_shape=pltpu.VMEM((copies, PACKET, LANES), jnp.float32),
+        out_shape=pltpu.VMEM((copies * PACKET, LANES), jnp.float32),
         in_specs=[smem] + [vmem] * 5,
         out_specs=vmem,
         scratch_shapes=[pltpu.VMEM((1, LANES), jnp.float32)],
         name="pack",
     )(owner.reshape(-1), estimate.reshape(SIDE, LANES), view_data.reshape(DATA_ROWS, LANES), taps_x, taps_y, taps_z)
-    ring = [(FIRST + j) % blocks for j in range(blocks)]
-    alike = [[(2 * g + c) * blocks + b for g in reversed(range(groups)) for b in ring] for c in range(2)]
-    near = lax.all_to_all(packet, ("view", "block"), 0, 0, axis_index_groups=alike, tiled=True)
+    alike = [
+        [(2 * g + (k ^ late(j))) * blocks + turned(j) for g in reversed(range(groups)) for j in range(blocks)]
+        for k in range(2)
+    ]
+    near = lax.all_to_all(
+        packet.reshape(copies, PACKET, 1, LANES), ("view", "block"), 0, 0, axis_index_groups=alike, tiled=True
+    )
     near = near.reshape(copies * PACKET, LANES)
     far = lax.ppermute(near, "view", [(v, v ^ 1) for v in range(views)])
-    near = pltpu.with_memory_space_constraint(near, pltpu.VMEM)
-    far = pltpu.with_memory_space_constraint(far, pltpu.VMEM)
+    wide = jnp.bfloat16
+    prepared = pl.pallas_call(
+        functools.partial(prepare_kernel, groups, width // 2),
+        out_shape=[
+            pltpu.VMEM((SIDE * SIDE, LANES), jnp.float32),
+            pltpu.VMEM((views, SIDE * SIDE, LANES), jnp.float32),
+            pltpu.VMEM((views, SIDE * SIDE, LANES), jnp.float32),
+            pltpu.VMEM((3 * LANES, views * LANES), wide),
+            pltpu.VMEM((views, SIDE * SIDE, 3 * SIDE * SIDE), wide),
+            pltpu.VMEM((views, SIDE * SIDE, 3 * SIDE * SIDE), wide),
+            pltpu.VMEM((3 * LANES, views * LANES), wide),
+        ],
+        in_specs=[vmem],
+        out_specs=[vmem] * 7,
+        name="prepare",
+    )(in_vmem(near))
     joined = pl.pallas_call(
-        functools.partial(volume_kernel, blocks, groups, reach),
+        functools.partial(finish_kernel, groups, width),
         out_shape=jax.ShapeDtypeStruct((SIDE, LANES), jnp.float32),
-        in_specs=[vmem] * 2,
+        in_specs=[vmem] * 8,
         out_specs=vmem,
         scratch_shapes=[pltpu.VMEM((SIDE * SIDE, LANES), jnp.float32)],
-        name="volume",
-    )(near, far)
+        name="finish",
+    )(in_vmem(far), *[in_vmem(value) for value in prepared])
     return joined.reshape(estimate.shape)
 
 

time: 18.3 us -> 16.9 us (0.923)
  blocking collectives: 13.6 us -> 11.8 us
  waiting for transfers between devices: 1.44 us -> 0.18 us
  starting transfers between devices: 0.01 us -> 1.19 us
  Pallas kernels: 3.09 us -> 3.48 us
    all_to_all x1, blocking collectives: 13.6 us -> 11.8 us  [on_device_small(): lax.all_to_all(packet.reshape(copies, PACKET, 1, LANES), ('view', 'block'...]
    ppermute x1, waiting for transfers between devices: 1.44 us -> 0.18 us  [on_device_small(): far = lax.ppermute(near, 'view', [(v, v ^ 1) for v in range(views)])]
    ppermute x1, starting transfers between devices: 0.01 us -> 1.19 us  [on_device_small(): far = lax.ppermute(near, 'view', [(v, v ^ 1) for v in range(views)])]
    pallas_call x1 -> x2, Pallas kernels: 2.2 us -> 2.59 us  [the longest x1 1.74 us: on_device_small(): pl.pallas_call(functools.partial(finish_kernel, groups, width), out_shape...]
  transfers between devices with their start and end apart: 1 -> 1, of which waited for: 1 -> 1; matrix products, arithmetic and copies ran while one was open for 0% -> 0% of each run, Pallas kernels for 0% -> 5%
where the time goes in v5:
time: 16.9 us; the launch traced here: 16.7 us
  blocking collectives  11.8 us (70%)
  Pallas kernels  3.48 us (21%)
  starting transfers between devices  1.19 us (7%)
  waiting for transfers between devices  0.18 us (1%)
    all_to_all x1, blocking collectives, on_device_small(): lax.all_to_all(packet.reshape(copies, PACKET, 1, LANES), ('view', 'block'...  11.8 us
    pallas_call x1, Pallas kernels, on_device_small(): pl.pallas_call(functools.partial(finish_kernel, groups, width), out_shape...  1.74 us
    ppermute x1, starting transfers between devices, on_device_small(): far = lax.ppermute(near, 'view', [(v, v ^ 1) for v in range(views)])  1.19 us
    pallas_call x1, Pallas kernels, on_device_small(): pl.pallas_call(functools.partial(pack_kernel, copies), out_shape=pltpu.VM...  0.88 us
    pallas_call x1, Pallas kernels, on_device_small(): pl.pallas_call(functools.partial(prepare_kernel, groups, width // 2), out...  0.85 us
  transfers between devices with their start and end apart: 1, of which 1 were waited for; matrix products, arithmetic and copies ran while one was open for 0% of the time, Pallas kernels for 5%

profile of v5, /device:TPU:0, one launch (start us, length us, event | category | flops | bytes accessed | tf_op | source)
XLA Modules:
  0.0 16.7 jit_solution(3660744340257522674)
XLA Ops:
  0.0 0.9 %pack.1 = f32[336,128]{1,0:T(8,128)S(1)} custom-call(s32[8]{0:T(128)} %bitcast.11, f32[8,128]{1,0:T(8,128)} %bitcast.10, f32[16,128]{1,0:T(8,128)} %bitcast.9, f32[1,33]{1,0:T(1,128)} %tx.1, f32[1,33]{1,0:T(1,128)} %ty.1, f32[1,33]{1,0:T(1,128)} %tz.1), custom_call_target="tpu_custom_call" | custom-call | tf_op jit(solution)/shard_map/pack/pallas_call | solution.py:197
  0.9 11.8 %all_to_all.5 = f32[16,21,1,128]{3,2,1,0:T(1,128)S(1)} all-to-all(f32[16,21,1,128]{3,2,1,0:T(1,128)S(1)} %bitcast.8), channel_id=1, replica_groups={{29,30,31,16,17,18,19,28,13,14,15,0,1,2,3,12},{21,22,23,24,25,26,27,20,..., dimensions={0} | all-to-all | bytes 344064 | tf_op jit(solution)/shard_map/all_to_all | solution.py:209
  12.7 1.2 %collective-permute-start = (f32[336,128]{1,0:T(8,128)S(1)}, f32[336,128]{1,0:T(8,128)S(1)}, u32[]{:S(2)}, u32[]{:S(2)}) collective-permute-start(f32[336,128]{1,0:T(8,128)S(1)} %bitcast.6), channel_id=1, source_target_pairs={{0,8},{8,0},{16,24},{24,16},{1,9},{9,1},{17,25},{25,17},{2,10},{10... | collective-permute-start | bytes 516104 | tf_op jit(solution)/shard_map/ppermute | solution.py:213
  13.9 0.8 %prepare.1 = (f32[64,128]{1,0:T(8,128)S(1)}, f32[4,64,128]{2,1,0:T(8,128)S(1)}, f32[4,64,128]{2,1,0:T(8,128)S(1)}, bf16[384,512]{1,0:T(8,128)(2,1)S(1)}, bf16[4,...) custom-call(f32[336,128]{1,0:T(8,128)S(1)} %bitcast.7), custom_call_target="tpu_custom_call" | custom-call | tf_op jit(solution)/shard_map/prepare/pallas_call | solution.py:215
  14.8 0.2 %collective-permute-done.far = f32[336,128]{1,0:T(8,128)S(1)} collective-permute-done((f32[336,128]{1,0:T(8,128)S(1)}, f32[336,128]{1,0:T(8,128)S(1)}, u32[]{:S(2)}, u32[]{:S(2)}) %collective-permute-start) | collective-permute-done | bytes 172064 | tf_op jit(solution)/shard_map/ppermute | solution.py:213
  14.9 1.7 %finish.1 = f32[8,128]{1,0:T(8,128)} custom-call(f32[336,128]{1,0:T(8,128)S(1)} %collective-permute-done.far, f32[64,128]{1,0:T(8,128)S(1)} %get-tuple-element.12.est_in, f32[4,64,128]{2,1,0:T(8,128)S(1)} %get-tuple-element.13.inverse, f32[4,64,128]{2,1,0:T(8,128)S(1)} %get-tuple-element.14.slabs_in, bf16[384,512]{1,0:T(8,128)(2,1)S(1)} %get-tuple-element.15.forward_depth, ...), custom_call_target="tpu_custom_call" | custom-call | tf_op jit(solution)/shard_map/finish/pallas_call | solution.py:230
Async XLA Ops:
  12.7 2.2 %collective-permute-start = (f32[336,128]{1,0:T(8,128)S(1)}, f32[336,128]{1,0:T(8,128)S(1)}, u32[]{:S(2)}, u32[]{:S(2)}) collective-permute-start(f32[336,128]{1,0:T(8,128)S(1)} %bitcast.6), channel_id=1, source_target_pairs={{0,8},{8,0},{16,24},{24,16},{1,9},{9,1},{17,25},{25,17},{2,10},{10... | collective-permute-start | bytes 516104 | tf_op jit(solution)/shard_map/ppermute | solution.py:213

commit v6 on v5

--- a/solution.py
+++ b/solution.py
@@ -18,10 +18,11 @@
 META = DATA_ROWS + EST_ROWS
 PACKET = META + 1
 FIRST = 5
+STEP = 3
 
 
 def turned(j):
-    return (j + FIRST) & (SIDE - 1)
+    return (STEP * j + FIRST) & (SIDE - 1)
 
 
 def late(j):
@@ -37,16 +38,14 @@
 
 
 def pack_kernel(copies, own, est, data, tx, ty, tz, out, meta):
-    block = lax.axis_index("block")
     group = lax.axis_index("view") >> 1
     width = tx.shape[1]
-    first = jnp.int32(-1)
-    second = jnp.int32(-1)
+    lane = lane_ids(1)
+    slots = jnp.zeros((1, LANES), jnp.int32)
     for y in range(SIDE):
-        mine = own[y] == block
-        second = jnp.where(mine & (first >= 0), y, second)
-        first = jnp.where(mine & (first < 0), y, first)
-    meta[...] = jnp.where(lane_ids(1) == 3 * width, first, second).astype(jnp.float32)
+        place = sum((own[c] == own[y]).astype(jnp.int32) for c in range(y))
+        slots = jnp.where(lane == 3 * width + y, 2 * own[y] + place, slots)
+    meta[...] = slots.astype(jnp.float32)
     for k, taps in enumerate((tx, ty, tz)):
         meta[:, k * width : (k + 1) * width] = taps[...]
     row = meta[...]
@@ -84,19 +83,18 @@
     return jnp.take_along_axis(tile, index, axis=1)
 
 
-def placed(slabs, ref, groups, width, flip):
-    for g in range(groups):
-        start = g * SIDE * PACKET
-        labels = ref[pl.ds(start + META, SIDE, stride=PACKET), :]
-        for s in range(2):
-            spread = lane_pick(labels, jnp.full((SIDE, LANES), 3 * width + s, jnp.int32))
-            for j in range(SIDE):
-                at = start + j * PACKET + s * SIDE
-                label = jnp.broadcast_to(spread[j : j + 1, :], (SIDE, LANES))
+def placed(slabs, ref, groups, slots, flip):
+    for v in range(2 * groups):
+        for j in [j for j in range(SIDE) if late(j) ^ flip == v // groups]:
+            for s in range(2):
+                at = ((v % groups) * SIDE + j) * PACKET + s * SIDE
                 slab = ref[at : at + SIDE, :]
-                mine = slabs[(late(j) ^ flip) * groups + g]
                 for y in range(SIDE):
-                    mine[y] = jnp.where(label == y, slab, mine[y])
+                    slabs[v][y] = jnp.where(slots[v][y] == 2 * turned(j) + s, slab, slabs[v][y])
+
+
+def spread_rows(tile):
+    return [jnp.broadcast_to(tile[y : y + 1, :], (SIDE, LANES)) for y in range(SIDE)]
 
 
 def blur(est, forward_depth, forward_side, views):
@@ -105,8 +103,11 @@
     return [matmul(forward_side[v], deep[v]) for v in views]
 
 
-def prepare_kernel(groups, reach, near, est_out, inverse, slabs_out, forward_depth, forward_side, back_side, back_depth):
+def prepare_kernel(
+    groups, reach, near, est_out, inverse, slabs_out, slots_out, forward_depth, forward_side, back_side, own_side, back_depth
+):
     width = 2 * reach + 1
+    block = lax.axis_index("block")
     views = range(2 * groups)
     tiles = []
     for y in range(SIDE):
@@ -135,36 +136,59 @@
         j = [late(j) for j in range(SIDE)].index(v // groups)
         at = ((v % groups) * SIDE + j) * PACKET + META
         metas.append(jnp.broadcast_to(near[at : at + 1, :], (SIDE, LANES)))
-    forward = [right(toeplitz(kernel_row(meta, 2, -signed))) for meta in metas]
-    sides = []
-    for v, meta in enumerate(metas):
-        for x_offset, y_offset, out in (
-            (turned(lane_x) - row, lane_y - row, forward_side),
-            (turned(row) - lane_x, row - lane_y, back_side),
-        ):
-            x_tile = kernel_row(meta, 0, x_offset)
-            y_tile = kernel_row(meta, 1, y_offset)
-            side = jnp.concatenate([x_tile * y_tile[y : y + 1, :] for y in range(SIDE)], axis=0)
-            side = left(side[:, : SIDE * SIDE])
-            out[v] = side
-            if out is forward_side:
-                sides.append(side)
-    forward = jnp.concatenate(forward, axis=1)
+    depth = [kernel_row(meta, 2, -signed) for meta in metas]
+    ahead = [
+        (kernel_row(meta, 0, turned(lane_x) - row), kernel_row(meta, 1, lane_y - row)) for meta in metas
+    ]
+    slots = [lane_pick(meta, row + 3 * width) for meta in metas]
+    depth_back = [kernel_row(meta, 2, signed) for meta in metas]
+    back_y = [kernel_row(meta, 1, row - lane_y) for meta in metas]
+    back_x = [kernel_row(meta, 0, turned(row) - lane_x) for meta in metas]
+    own_x = [kernel_row(meta, 0, block - lane_x) for meta in metas]
+
+    def side_matrix(x_tile, y_tile):
+        side = jnp.concatenate([x_tile * y_row for y_row in spread_rows(y_tile)], axis=0)
+        return left(side[:, : SIDE * SIDE])
+
+    forward = jnp.concatenate([right(toeplitz(base)) for base in depth], axis=1)
+    sides = [side_matrix(x_tile, y_tile) for x_tile, y_tile in ahead]
+    blurred = blur(est, forward, sides, views)
+    slots = [spread_rows(tile) for tile in slots]
+    slabs = [[jnp.zeros((SIDE, LANES), jnp.float32)] * SIDE for _ in views]
+    placed(slabs, near, groups, slots, 0)
     forward_depth[...] = forward
-    blurred = blur(est, forward, sides, views)
-    slabs = [[jnp.zeros((SIDE, LANES), jnp.float32)] * SIDE for _ in views]
-    placed(slabs, near, groups, width, 0)
-    for v, meta in enumerate(metas):
-        back_depth[:, v * LANES : (v + 1) * LANES] = right(toeplitz(kernel_row(meta, 2, signed)))
+    for v in views:
+        forward_side[v] = sides[v]
+        back_side[v] = side_matrix(back_x[v], back_y[v])
+        own = own_x[v] * back_y[v]
+        own_side[v] = left(jnp.concatenate([own, own], axis=0)[:, : SIDE * SIDE])
+        back_depth[:, v * LANES : (v + 1) * LANES] = right(toeplitz(depth_back[v]))
         slabs_out[v] = jnp.concatenate(slabs[v], axis=0)
+        slots_out[v] = jnp.concatenate(slots[v], axis=0)
+    for v in views:
         inverse[v] = 1.0 / blurred[v]
 
 
-def finish_kernel(groups, width, far, est_in, inverse, slabs_in, forward_depth, forward_side, back_side, back_depth, out, held):
+def finish_kernel(
+    groups,
+    far,
+    est_in,
+    inverse,
+    slabs_in,
+    slots_in,
+    forward_depth,
+    forward_side,
+    back_side,
+    own_side,
+    back_depth,
+    out,
+    held,
+):
     block = lax.axis_index("block")
     views = range(2 * groups)
     slabs = [[slabs_in[v, y * SIDE : (y + 1) * SIDE, :] for y in range(SIDE)] for v in views]
-    placed(slabs, far, groups, width, 1)
+    slots = [[slots_in[v, y * SIDE : (y + 1) * SIDE, :] for y in range(SIDE)] for v in views]
+    placed(slabs, far, groups, slots, 1)
     recorded = [jnp.concatenate(slabs[v], axis=0) for v in views]
     est = est_in[...]
     for step in range(ITERS):
@@ -174,12 +198,17 @@
             blurred = blur(est, forward_depth[...], [forward_side[v] for v in views], views)
             ratios = [recorded[v] / blurred[v] for v in views]
         ratios = [right(ratios[v]) for v in views]
-        spread = [left(matmul(back_side[v], ratios[v])) for v in views]
+        last = step == ITERS - 1
+        back = own_side if last else back_side
+        spread = [left(matmul(back[v], ratios[v])) for v in views]
         corr = [matmul(spread[v], back_depth[:, v * LANES : (v + 1) * LANES]) for v in views]
+        if last:
+            corr = [value[:SIDE] for value in corr]
+            held[...] = est
+            est = held[pl.ds((STEP * (block - FIRST)) & (SIDE - 1), SIDE, stride=SIDE), :]
         roots = [lax.rsqrt(corr[v] * corr[v + 1]) for v in views[::2]]
         est = est * lax.rsqrt(roots[0] * roots[1])
-    held[...] = est
-    out[...] = held[pl.ds((block - FIRST) & (SIDE - 1), SIDE, stride=SIDE), :]
+    out[...] = est
 
 
 def in_vmem(value):
@@ -218,19 +247,21 @@
             pltpu.VMEM((SIDE * SIDE, LANES), jnp.float32),
             pltpu.VMEM((views, SIDE * SIDE, LANES), jnp.float32),
             pltpu.VMEM((views, SIDE * SIDE, LANES), jnp.float32),
+            pltpu.VMEM((views, SIDE * SIDE, LANES), jnp.float32),
             pltpu.VMEM((3 * LANES, views * LANES), wide),
             pltpu.VMEM((views, SIDE * SIDE, 3 * SIDE * SIDE), wide),
             pltpu.VMEM((views, SIDE * SIDE, 3 * SIDE * SIDE), wide),
+            pltpu.VMEM((views, 2 * SIDE, 3 * SIDE * SIDE), wide),
             pltpu.VMEM((3 * LANES, views * LANES), wide),
         ],
         in_specs=[vmem],
-        out_specs=[vmem] * 7,
+        out_specs=[vmem] * 9,
         name="prepare",
     )(in_vmem(near))
     joined = pl.pallas_call(
-        functools.partial(finish_kernel, groups, width),
+        functools.partial(finish_kernel, groups),
         out_shape=jax.ShapeDtypeStruct((SIDE, LANES), jnp.float32),
-        in_specs=[vmem] * 8,
+        in_specs=[vmem] * 10,
         out_specs=vmem,
         scratch_shapes=[pltpu.VMEM((SIDE * SIDE, LANES), jnp.float32)],
         name="finish",
@@ -245,7 +276,7 @@
         and view_data.shape[1] == 2
         and views == 4
         and taps_x.shape[1] % 2 == 1
-        and 3 * taps_x.shape[1] + 2 <= LANES
+        and 3 * taps_x.shape[1] + SIDE <= LANES
     )
 
 

time: 16.9 us -> 16.5 us (0.976)
  Pallas kernels: 3.48 us -> 3.08 us
  waiting for transfers between devices: 0.18 us -> 0.44 us
    pallas_call x1, Pallas kernels: 0.85 us -> 0.59 us  [on_device_small(): pl.pallas_call(functools.partial(prepare_kernel, groups, width // 2), out...]
    ppermute x1, waiting for transfers between devices: 0.18 us -> 0.44 us  [on_device_small(): far = lax.ppermute(near, 'view', [(v, v ^ 1) for v in range(views)])]
  transfers between devices with their start and end apart: 1 -> 1, of which waited for: 1 -> 1; matrix products, arithmetic and copies ran while one was open for 0% -> 0% of each run, Pallas kernels for 5% -> 4%
where the time goes in v6:
time: 16.5 us; the launch traced here: 16.4 us
  blocking collectives  11.7 us (71%)
  Pallas kernels  3.08 us (19%)
  starting transfers between devices  1.15 us (7%)
  waiting for transfers between devices  0.44 us (3%)
    all_to_all x1, blocking collectives, on_device_small(): lax.all_to_all(packet.reshape(copies, PACKET, 1, LANES), ('view', 'block'...  11.7 us
    pallas_call x1, Pallas kernels, on_device_small(): pl.pallas_call(functools.partial(finish_kernel, groups), out_shape=jax.Sh...  1.6 us
    ppermute x1, starting transfers between devices, on_device_small(): far = lax.ppermute(near, 'view', [(v, v ^ 1) for v in range(views)])  1.15 us
    pallas_call x1, Pallas kernels, on_device_small(): pl.pallas_call(functools.partial(pack_kernel, copies), out_shape=pltpu.VM...  0.88 us
    pallas_call x1, Pallas kernels, on_device_small(): pl.pallas_call(functools.partial(prepare_kernel, groups, width // 2), out...  0.59 us
    ppermute x1, waiting for transfers between devices, on_device_small(): far = lax.ppermute(near, 'view', [(v, v ^ 1) for v in range(views)])  0.44 us
  transfers between devices with their start and end apart: 1, of which 1 were waited for; matrix products, arithmetic and copies ran while one was open for 0% of the time, Pallas kernels for 4%

profile of v6, /device:TPU:0, one launch (start us, length us, event | category | flops | bytes accessed | tf_op | source)
XLA Modules:
  0.0 16.4 jit_solution(5639754919924075732)
XLA Ops:
  0.0 0.9 %pack.1 = f32[336,128]{1,0:T(8,128)S(1)} custom-call(s32[8]{0:T(128)} %bitcast.11, f32[8,128]{1,0:T(8,128)} %bitcast.10, f32[16,128]{1,0:T(8,128)} %bitcast.9, f32[1,33]{1,0:T(1,128)} %tx.1, f32[1,33]{1,0:T(1,128)} %ty.1, f32[1,33]{1,0:T(1,128)} %tz.1), custom_call_target="tpu_custom_call" | custom-call | tf_op jit(solution)/shard_map/pack/pallas_call | solution.py:226
  0.9 11.7 %all_to_all.5 = f32[16,21,1,128]{3,2,1,0:T(1,128)S(1)} all-to-all(f32[16,21,1,128]{3,2,1,0:T(1,128)S(1)} %bitcast.8), channel_id=1, replica_groups={{29,16,19,30,17,28,31,18,13,0,3,14,1,12,15,2},{21,24,27,22,25,20,23,26,..., dimensions={0} | all-to-all | bytes 344064 | tf_op jit(solution)/shard_map/all_to_all | solution.py:238
  12.6 1.2 %collective-permute-start = (f32[336,128]{1,0:T(8,128)S(1)}, f32[336,128]{1,0:T(8,128)S(1)}, u32[]{:S(2)}, u32[]{:S(2)}) collective-permute-start(f32[336,128]{1,0:T(8,128)S(1)} %bitcast.6), channel_id=1, source_target_pairs={{0,8},{8,0},{16,24},{24,16},{1,9},{9,1},{17,25},{25,17},{2,10},{10... | collective-permute-start | bytes 516104 | tf_op jit(solution)/shard_map/ppermute | solution.py:242
  13.7 0.6 %prepare.1 = (f32[64,128]{1,0:T(8,128)S(1)}, f32[4,64,128]{2,1,0:T(8,128)S(1)}, f32[4,64,128]{2,1,0:T(8,128)S(1)}, f32[4,64,128]{2,1,0:T(8,128)S(1)}, bf16[384,5...) custom-call(f32[336,128]{1,0:T(8,128)S(1)} %bitcast.7), custom_call_target="tpu_custom_call" | custom-call | tf_op jit(solution)/shard_map/prepare/pallas_call | solution.py:244
  14.3 0.4 %collective-permute-done.far = f32[336,128]{1,0:T(8,128)S(1)} collective-permute-done((f32[336,128]{1,0:T(8,128)S(1)}, f32[336,128]{1,0:T(8,128)S(1)}, u32[]{:S(2)}, u32[]{:S(2)}) %collective-permute-start) | collective-permute-done | bytes 172064 | tf_op jit(solution)/shard_map/ppermute | solution.py:242
  14.7 1.6 %finish.1 = f32[8,128]{1,0:T(8,128)} custom-call(f32[336,128]{1,0:T(8,128)S(1)} %collective-permute-done.far, f32[64,128]{1,0:T(8,128)S(1)} %get-tuple-element.14.est_in, f32[4,64,128]{2,1,0:T(8,128)S(1)} %get-tuple-element.15.inverse, f32[4,64,128]{2,1,0:T(8,128)S(1)} %get-tuple-element.16.slabs_in, f32[4,64,128]{2,1,0:T(8,128)S(1)} %get-tuple-element.17.slots_in, ...), custom_call_target="tpu_custom_call" | custom-call | tf_op jit(solution)/shard_map/finish/pallas_call | solution.py:261
Async XLA Ops:
  12.6 2.2 %collective-permute-start = (f32[336,128]{1,0:T(8,128)S(1)}, f32[336,128]{1,0:T(8,128)S(1)}, u32[]{:S(2)}, u32[]{:S(2)}) collective-permute-start(f32[336,128]{1,0:T(8,128)S(1)} %bitcast.6), channel_id=1, source_target_pairs={{0,8},{8,0},{16,24},{24,16},{1,9},{9,1},{17,25},{25,17},{2,10},{10... | collective-permute-start | bytes 516104 | tf_op jit(solution)/shard_map/ppermute | solution.py:242

commit v7 on v6

--- a/solution.py
+++ b/solution.py
@@ -17,16 +17,11 @@
 EST_ROWS = 4
 META = DATA_ROWS + EST_ROWS
 PACKET = META + 1
-FIRST = 5
-STEP = 3
-
-
-def turned(j):
-    return (STEP * j + FIRST) & (SIDE - 1)
-
-
-def late(j):
-    return int(turned(j) >= SIDE // 2)
+ORDER = (
+    *((1, 5), (0, 2), (0, 1), (0, 6), (1, 1), (1, 2), (0, 4), (1, 4)),
+    *((0, 5), (1, 0), (0, 7), (0, 0), (1, 3), (1, 6), (0, 3), (1, 7)),
+)
+LATE = {(g, b): int(b >= 4) for g, b in ORDER}
 
 
 def lane_ids(rows):
@@ -40,12 +35,8 @@
 def pack_kernel(copies, own, est, data, tx, ty, tz, out, meta):
     group = lax.axis_index("view") >> 1
     width = tx.shape[1]
-    lane = lane_ids(1)
-    slots = jnp.zeros((1, LANES), jnp.int32)
-    for y in range(SIDE):
-        place = sum((own[c] == own[y]).astype(jnp.int32) for c in range(y))
-        slots = jnp.where(lane == 3 * width + y, 2 * own[y] + place, slots)
-    meta[...] = slots.astype(jnp.float32)
+    meta[...] = jnp.zeros_like(meta)
+    meta[:, 3 * width : 3 * width + SIDE] = own[...].astype(jnp.float32)
     for k, taps in enumerate((tx, ty, tz)):
         meta[:, k * width : (k + 1) * width] = taps[...]
     row = meta[...]
@@ -84,13 +75,23 @@
 
 
 def placed(slabs, ref, groups, slots, flip):
-    for v in range(2 * groups):
-        for j in [j for j in range(SIDE) if late(j) ^ flip == v // groups]:
-            for s in range(2):
-                at = ((v % groups) * SIDE + j) * PACKET + s * SIDE
-                slab = ref[at : at + SIDE, :]
-                for y in range(SIDE):
-                    slabs[v][y] = jnp.where(slots[v][y] == 2 * turned(j) + s, slab, slabs[v][y])
+    for p, (g, b) in enumerate(ORDER):
+        v = (LATE[g, b] ^ flip) * groups + g
+        for s in range(2):
+            at = p * PACKET + s * SIDE
+            slab = ref[at : at + SIDE, :]
+            for y in range(SIDE):
+                slabs[v][y] = jnp.where(slots[v][y] == 2 * b + s, slab, slabs[v][y])
+
+
+def slot_numbers(owners):
+    numbers = []
+    for y, mine in enumerate(owners):
+        place = jnp.zeros_like(mine)
+        for other in owners[:y]:
+            place += jnp.where(other == mine, 1.0, 0.0)
+        numbers.append(2.0 * mine + place)
+    return numbers
 
 
 def spread_rows(tile):
@@ -109,12 +110,11 @@
     width = 2 * reach + 1
     block = lax.axis_index("block")
     views = range(2 * groups)
-    tiles = []
-    for y in range(SIDE):
-        start = (groups - 1 - y // EST_ROWS) * SIDE * PACKET + DATA_ROWS + y % EST_ROWS
-        tiles.append(near[pl.ds(start, SIDE, stride=PACKET), :])
-    est = jnp.concatenate(tiles, axis=0)
-    est_out[...] = est
+    for p, (g, b) in enumerate(ORDER):
+        for i in range(EST_ROWS):
+            y, at = g * EST_ROWS + i, p * PACKET + DATA_ROWS + i
+            est_out[y * SIDE + b : y * SIDE + b + 1, :] = near[at : at + 1, :]
+    est = est_out[...]
 
     lane, row = lane_ids(SIDE), row_ids(SIDE)
     lane_x, lane_y = lane & (SIDE - 1), lane >> 3
@@ -133,17 +133,17 @@
 
     metas = []
     for v in views:
-        j = [late(j) for j in range(SIDE)].index(v // groups)
-        at = ((v % groups) * SIDE + j) * PACKET + META
+        p = [(LATE[key], key[0]) for key in ORDER].index((v // groups, v % groups))
+        at = p * PACKET + META
         metas.append(jnp.broadcast_to(near[at : at + 1, :], (SIDE, LANES)))
     depth = [kernel_row(meta, 2, -signed) for meta in metas]
     ahead = [
-        (kernel_row(meta, 0, turned(lane_x) - row), kernel_row(meta, 1, lane_y - row)) for meta in metas
+        (kernel_row(meta, 0, lane_x - row), kernel_row(meta, 1, lane_y - row)) for meta in metas
     ]
-    slots = [lane_pick(meta, row + 3 * width) for meta in metas]
+    owners = [lane_pick(meta, row + 3 * width) for meta in metas]
     depth_back = [kernel_row(meta, 2, signed) for meta in metas]
     back_y = [kernel_row(meta, 1, row - lane_y) for meta in metas]
-    back_x = [kernel_row(meta, 0, turned(row) - lane_x) for meta in metas]
+    back_x = [kernel_row(meta, 0, row - lane_x) for meta in metas]
     own_x = [kernel_row(meta, 0, block - lane_x) for meta in metas]
 
     def side_matrix(x_tile, y_tile):
@@ -153,7 +153,7 @@
     forward = jnp.concatenate([right(toeplitz(base)) for base in depth], axis=1)
     sides = [side_matrix(x_tile, y_tile) for x_tile, y_tile in ahead]
     blurred = blur(est, forward, sides, views)
-    slots = [spread_rows(tile) for tile in slots]
+    slots = [slot_numbers(spread_rows(tile)) for tile in owners]
     slabs = [[jnp.zeros((SIDE, LANES), jnp.float32)] * SIDE for _ in views]
     placed(slabs, near, groups, slots, 0)
     forward_depth[...] = forward
@@ -205,7 +205,7 @@
         if last:
             corr = [value[:SIDE] for value in corr]
             held[...] = est
-            est = held[pl.ds((STEP * (block - FIRST)) & (SIDE - 1), SIDE, stride=SIDE), :]
+            est = held[pl.ds(block, SIDE, stride=SIDE), :]
         roots = [lax.rsqrt(corr[v] * corr[v + 1]) for v in views[::2]]
         est = est * lax.rsqrt(roots[0] * roots[1])
     out[...] = est
@@ -221,20 +221,16 @@
     width = taps_x.shape[1]
     groups = views // 2
     copies = groups * blocks
-    smem = pl.BlockSpec(memory_space=pltpu.SMEM)
     vmem = pl.BlockSpec(memory_space=pltpu.VMEM)
     packet = pl.pallas_call(
         functools.partial(pack_kernel, copies),
         out_shape=pltpu.VMEM((copies * PACKET, LANES), jnp.float32),
-        in_specs=[smem] + [vmem] * 5,
+        in_specs=[vmem] * 6,
         out_specs=vmem,
         scratch_shapes=[pltpu.VMEM((1, LANES), jnp.float32)],
         name="pack",
-    )(owner.reshape(-1), estimate.reshape(SIDE, LANES), view_data.reshape(DATA_ROWS, LANES), taps_x, taps_y, taps_z)
-    alike = [
-        [(2 * g + (k ^ late(j))) * blocks + turned(j) for g in reversed(range(groups)) for j in range(blocks)]
-        for k in range(2)
-    ]
+    )(owner.reshape(1, SIDE), estimate.reshape(SIDE, LANES), view_data.reshape(DATA_ROWS, LANES), taps_x, taps_y, taps_z)
+    alike = [[(2 * g + (k ^ LATE[g, b])) * blocks + b for g, b in ORDER] for k in range(2)]
     near = lax.all_to_all(
         packet.reshape(copies, PACKET, 1, LANES), ("view", "block"), 0, 0, axis_index_groups=alike, tiled=True
     )

time: 16.5 us -> 16.1 us (0.976)
  starting transfers between devices: 1.15 us -> 0.75 us
    ppermute x1, starting transfers between devices: 1.15 us -> 0.75 us  [on_device_small(): far = lax.ppermute(near, 'view', [(v, v ^ 1) for v in range(views)])]
where the time goes in v7:
time: 16.1 us; the launch traced here: 15.9 us
  blocking collectives  11.7 us (73%)
  Pallas kernels  3.08 us (19%)
  starting transfers between devices  0.75 us (5%)
  waiting for transfers between devices  0.39 us (2%)
    all_to_all x1, blocking collectives, on_device_small(): lax.all_to_all(packet.reshape(copies, PACKET, 1, LANES), ('view', 'block'...  11.7 us
    pallas_call x1, Pallas kernels, on_device_small(): pl.pallas_call(functools.partial(finish_kernel, groups), out_shape=jax.Sh...  1.61 us
    pallas_call x1, Pallas kernels, on_device_small(): pl.pallas_call(functools.partial(pack_kernel, copies), out_shape=pltpu.VM...  0.83 us
    ppermute x1, starting transfers between devices, on_device_small(): far = lax.ppermute(near, 'view', [(v, v ^ 1) for v in range(views)])  0.75 us
    pallas_call x1, Pallas kernels, on_device_small(): pl.pallas_call(functools.partial(prepare_kernel, groups, width // 2), out...  0.64 us
    ppermute x1, waiting for transfers between devices, on_device_small(): far = lax.ppermute(near, 'view', [(v, v ^ 1) for v in range(views)])  0.39 us
  transfers between devices with their start and end apart: 1, of which 1 were waited for; matrix products, arithmetic and copies ran while one was open for 0% of the time, Pallas kernels for 4%

profile of v7, /device:TPU:0, one launch (start us, length us, event | category | flops | bytes accessed | tf_op | source)
XLA Modules:
  0.0 15.9 jit_solution(14741163024075922454)
XLA Ops:
  0.0 0.8 %pack.1 = f32[336,128]{1,0:T(8,128)S(1)} custom-call(s32[1,8]{1,0:T(1,128)} %bitcast.11, f32[8,128]{1,0:T(8,128)} %bitcast.10, f32[16,128]{1,0:T(8,128)} %bitcast.9, f32[1,33]{1,0:T(1,128)} %tx.1, f32[1,33]{1,0:T(1,128)} %ty.1, f32[1,33]{1,0:T(1,128)} %tz.1), custom_call_target="tpu_custom_call" | custom-call | tf_op jit(solution)/shard_map/pack/pallas_call | solution.py:225
  0.8 11.7 %all_to_all.5 = f32[16,21,1,128]{3,2,1,0:T(1,128)S(1)} all-to-all(f32[16,21,1,128]{3,2,1,0:T(1,128)S(1)} %bitcast.8), channel_id=1, replica_groups={{29,2,1,14,17,18,12,28,13,16,15,0,19,30,3,31},{21,10,9,6,25,26,4,20,5,2..., dimensions={0} | all-to-all | bytes 344064 | tf_op jit(solution)/shard_map/all_to_all | solution.py:234
  12.6 0.7 %collective-permute-start = (f32[336,128]{1,0:T(8,128)S(1)}, f32[336,128]{1,0:T(8,128)S(1)}, u32[]{:S(2)}, u32[]{:S(2)}) collective-permute-start(f32[336,128]{1,0:T(8,128)S(1)} %bitcast.6), channel_id=1, source_target_pairs={{0,8},{8,0},{16,24},{24,16},{1,9},{9,1},{17,25},{25,17},{2,10},{10... | collective-permute-start | bytes 516104 | tf_op jit(solution)/shard_map/ppermute | solution.py:238
  13.3 0.6 %prepare.1 = (f32[64,128]{1,0:T(8,128)S(1)}, f32[4,64,128]{2,1,0:T(8,128)S(1)}, f32[4,64,128]{2,1,0:T(8,128)S(1)}, f32[4,64,128]{2,1,0:T(8,128)S(1)}, bf16[384,5...) custom-call(f32[336,128]{1,0:T(8,128)S(1)} %bitcast.7), custom_call_target="tpu_custom_call" | custom-call | tf_op jit(solution)/shard_map/prepare/pallas_call | solution.py:240
  13.9 0.4 %collective-permute-done.far = f32[336,128]{1,0:T(8,128)S(1)} collective-permute-done((f32[336,128]{1,0:T(8,128)S(1)}, f32[336,128]{1,0:T(8,128)S(1)}, u32[]{:S(2)}, u32[]{:S(2)}) %collective-permute-start) | collective-permute-done | bytes 172064 | tf_op jit(solution)/shard_map/ppermute | solution.py:238
  14.3 1.6 %finish.1 = f32[8,128]{1,0:T(8,128)} custom-call(f32[336,128]{1,0:T(8,128)S(1)} %collective-permute-done.far, f32[64,128]{1,0:T(8,128)S(1)} %get-tuple-element.14.est_in, f32[4,64,128]{2,1,0:T(8,128)S(1)} %get-tuple-element.15.inverse, f32[4,64,128]{2,1,0:T(8,128)S(1)} %get-tuple-element.16.slabs_in, f32[4,64,128]{2,1,0:T(8,128)S(1)} %get-tuple-element.17.slots_in, ...), custom_call_target="tpu_custom_call" | custom-call | tf_op jit(solution)/shard_map/finish/pallas_call | solution.py:257
Async XLA Ops:
  12.6 1.8 %collective-permute-start = (f32[336,128]{1,0:T(8,128)S(1)}, f32[336,128]{1,0:T(8,128)S(1)}, u32[]{:S(2)}, u32[]{:S(2)}) collective-permute-start(f32[336,128]{1,0:T(8,128)S(1)} %bitcast.6), channel_id=1, source_target_pairs={{0,8},{8,0},{16,24},{24,16},{1,9},{9,1},{17,25},{25,17},{2,10},{10... | collective-permute-start | bytes 516104 | tf_op jit(solution)/shard_map/ppermute | solution.py:238

commit v8 on v7

--- a/solution.py
+++ b/solution.py
@@ -204,7 +204,7 @@
         corr = [matmul(spread[v], back_depth[:, v * LANES : (v + 1) * LANES]) for v in views]
         if last:
             corr = [value[:SIDE] for value in corr]
-            held[...] = est
+            held[: SIDE * SIDE, :] = est
             est = held[pl.ds(block, SIDE, stride=SIDE), :]
         roots = [lax.rsqrt(corr[v] * corr[v + 1]) for v in views[::2]]
         est = est * lax.rsqrt(roots[0] * roots[1])
@@ -259,7 +259,7 @@
         out_shape=jax.ShapeDtypeStruct((SIDE, LANES), jnp.float32),
         in_specs=[vmem] * 10,
         out_specs=vmem,
-        scratch_shapes=[pltpu.VMEM((SIDE * SIDE, LANES), jnp.float32)],
+        scratch_shapes=[pltpu.VMEM((2 * SIDE * SIDE, LANES), jnp.float32)],
         name="finish",
     )(in_vmem(far), *[in_vmem(value) for value in prepared])
     return joined.reshape(estimate.shape)

time: 16.1 us -> 16.1 us (level)
  no operation moved by 1% of the time
where the time goes in v8:
time: 16.1 us; the launch traced here: 15.9 us
  blocking collectives  11.7 us (73%)
  Pallas kernels  3.08 us (19%)
  starting transfers between devices  0.75 us (5%)
  waiting for transfers between devices  0.39 us (2%)
    all_to_all x1, blocking collectives, on_device_small(): lax.all_to_all(packet.reshape(copies, PACKET, 1, LANES), ('view', 'block'...  11.7 us
    pallas_call x1, Pallas kernels, on_device_small(): pl.pallas_call(functools.partial(finish_kernel, groups), out_shape=jax.Sh...  1.61 us
    pallas_call x1, Pallas kernels, on_device_small(): pl.pallas_call(functools.partial(pack_kernel, copies), out_shape=pltpu.VM...  0.83 us
    ppermute x1, starting transfers between devices, on_device_small(): far = lax.ppermute(near, 'view', [(v, v ^ 1) for v in range(views)])  0.75 us
    pallas_call x1, Pallas kernels, on_device_small(): pl.pallas_call(functools.partial(prepare_kernel, groups, width // 2), out...  0.64 us
    ppermute x1, waiting for transfers between devices, on_device_small(): far = lax.ppermute(near, 'view', [(v, v ^ 1) for v in range(views)])  0.39 us
  transfers between devices with their start and end apart: 1, of which 1 were waited for; matrix products, arithmetic and copies ran while one was open for 0% of the time, Pallas kernels for 4%

profile of v8, /device:TPU:0, one launch (start us, length us, event | category | flops | bytes accessed | tf_op | source)
XLA Modules:
  0.0 15.9 jit_solution(17617830529760636416)
XLA Ops:
  0.0 0.8 %pack.1 = f32[336,128]{1,0:T(8,128)S(1)} custom-call(s32[1,8]{1,0:T(1,128)} %bitcast.11, f32[8,128]{1,0:T(8,128)} %bitcast.10, f32[16,128]{1,0:T(8,128)} %bitcast.9, f32[1,33]{1,0:T(1,128)} %tx.1, f32[1,33]{1,0:T(1,128)} %ty.1, f32[1,33]{1,0:T(1,128)} %tz.1), custom_call_target="tpu_custom_call" | custom-call | tf_op jit(solution)/shard_map/pack/pallas_call | solution.py:225
  0.8 11.7 %all_to_all.5 = f32[16,21,1,128]{3,2,1,0:T(1,128)S(1)} all-to-all(f32[16,21,1,128]{3,2,1,0:T(1,128)S(1)} %bitcast.8), channel_id=1, replica_groups={{29,2,1,14,17,18,12,28,13,16,15,0,19,30,3,31},{21,10,9,6,25,26,4,20,5,2..., dimensions={0} | all-to-all | bytes 344064 | tf_op jit(solution)/shard_map/all_to_all | solution.py:234
  12.6 0.7 %collective-permute-start = (f32[336,128]{1,0:T(8,128)S(1)}, f32[336,128]{1,0:T(8,128)S(1)}, u32[]{:S(2)}, u32[]{:S(2)}) collective-permute-start(f32[336,128]{1,0:T(8,128)S(1)} %bitcast.6), channel_id=1, source_target_pairs={{0,8},{8,0},{16,24},{24,16},{1,9},{9,1},{17,25},{25,17},{2,10},{10... | collective-permute-start | bytes 516104 | tf_op jit(solution)/shard_map/ppermute | solution.py:238
  13.3 0.6 %prepare.1 = (f32[64,128]{1,0:T(8,128)S(1)}, f32[4,64,128]{2,1,0:T(8,128)S(1)}, f32[4,64,128]{2,1,0:T(8,128)S(1)}, f32[4,64,128]{2,1,0:T(8,128)S(1)}, bf16[384,5...) custom-call(f32[336,128]{1,0:T(8,128)S(1)} %bitcast.7), custom_call_target="tpu_custom_call" | custom-call | tf_op jit(solution)/shard_map/prepare/pallas_call | solution.py:240
  13.9 0.4 %collective-permute-done.far = f32[336,128]{1,0:T(8,128)S(1)} collective-permute-done((f32[336,128]{1,0:T(8,128)S(1)}, f32[336,128]{1,0:T(8,128)S(1)}, u32[]{:S(2)}, u32[]{:S(2)}) %collective-permute-start) | collective-permute-done | bytes 172064 | tf_op jit(solution)/shard_map/ppermute | solution.py:238
  14.3 1.6 %finish.1 = f32[8,128]{1,0:T(8,128)} custom-call(f32[336,128]{1,0:T(8,128)S(1)} %collective-permute-done.far, f32[64,128]{1,0:T(8,128)S(1)} %get-tuple-element.14.est_in, f32[4,64,128]{2,1,0:T(8,128)S(1)} %get-tuple-element.15.inverse, f32[4,64,128]{2,1,0:T(8,128)S(1)} %get-tuple-element.16.slabs_in, f32[4,64,128]{2,1,0:T(8,128)S(1)} %get-tuple-element.17.slots_in, ...), custom_call_target="tpu_custom_call" | custom-call | tf_op jit(solution)/shard_map/finish/pallas_call | solution.py:257
Async XLA Ops:
  12.6 1.8 %collective-permute-start = (f32[336,128]{1,0:T(8,128)S(1)}, f32[336,128]{1,0:T(8,128)S(1)}, u32[]{:S(2)}, u32[]{:S(2)}) collective-permute-start(f32[336,128]{1,0:T(8,128)S(1)} %bitcast.6), channel_id=1, source_target_pairs={{0,8},{8,0},{16,24},{24,16},{1,9},{9,1},{17,25},{25,17},{2,10},{10... | collective-permute-start | bytes 516104 | tf_op jit(solution)/shard_map/ppermute | solution.py:238

commit v9 on v8

--- a/solution.py
+++ b/solution.py
@@ -74,11 +74,11 @@
     return jnp.take_along_axis(tile, index, axis=1)
 
 
-def placed(slabs, ref, groups, slots, flip):
+def placed(slabs, ref, length, groups, slots, flip):
     for p, (g, b) in enumerate(ORDER):
         v = (LATE[g, b] ^ flip) * groups + g
         for s in range(2):
-            at = p * PACKET + s * SIDE
+            at = p * length + s * SIDE
             slab = ref[at : at + SIDE, :]
             for y in range(SIDE):
                 slabs[v][y] = jnp.where(slots[v][y] == 2 * b + s, slab, slabs[v][y])
@@ -155,7 +155,7 @@
     blurred = blur(est, forward, sides, views)
     slots = [slot_numbers(spread_rows(tile)) for tile in owners]
     slabs = [[jnp.zeros((SIDE, LANES), jnp.float32)] * SIDE for _ in views]
-    placed(slabs, near, groups, slots, 0)
+    placed(slabs, near, PACKET, groups, slots, 0)
     forward_depth[...] = forward
     for v in views:
         forward_side[v] = sides[v]
@@ -188,7 +188,7 @@
     views = range(2 * groups)
     slabs = [[slabs_in[v, y * SIDE : (y + 1) * SIDE, :] for y in range(SIDE)] for v in views]
     slots = [[slots_in[v, y * SIDE : (y + 1) * SIDE, :] for y in range(SIDE)] for v in views]
-    placed(slabs, far, groups, slots, 1)
+    placed(slabs, far, DATA_ROWS, groups, slots, 1)
     recorded = [jnp.concatenate(slabs[v], axis=0) for v in views]
     est = est_in[...]
     for step in range(ITERS):
@@ -234,8 +234,9 @@
     near = lax.all_to_all(
         packet.reshape(copies, PACKET, 1, LANES), ("view", "block"), 0, 0, axis_index_groups=alike, tiled=True
     )
+    far = near[:, :DATA_ROWS].reshape(copies * DATA_ROWS, LANES)
+    far = lax.ppermute(far, "view", [(v, v ^ 1) for v in range(views)])
     near = near.reshape(copies * PACKET, LANES)
-    far = lax.ppermute(near, "view", [(v, v ^ 1) for v in range(views)])
     wide = jnp.bfloat16
     prepared = pl.pallas_call(
         functools.partial(prepare_kernel, groups, width // 2),

time: 16.1 us -> 16.2 us (level)
  no operation moved by 1% of the time
where the time goes in v9:
time: 16.2 us; the launch traced here: 16 us
  blocking collectives  11.7 us (72%)
  Pallas kernels  3.08 us (19%)
  starting transfers between devices  0.81 us (5%)
  waiting for transfers between devices  0.34 us (2%)
    all_to_all x1, blocking collectives, on_device_small(): lax.all_to_all(packet.reshape(copies, PACKET, 1, LANES), ('view', 'block'...  11.7 us
    pallas_call x1, Pallas kernels, on_device_small(): pl.pallas_call(functools.partial(finish_kernel, groups), out_shape=jax.Sh...  1.6 us
    pallas_call x1, Pallas kernels, on_device_small(): pl.pallas_call(functools.partial(pack_kernel, copies), out_shape=pltpu.VM...  0.83 us
    ppermute x1, starting transfers between devices, on_device_small(): far = lax.ppermute(far, 'view', [(v, v ^ 1) for v in range(views)])  0.81 us
    pallas_call x1, Pallas kernels, on_device_small(): pl.pallas_call(functools.partial(prepare_kernel, groups, width // 2), out...  0.64 us
    ppermute x1, waiting for transfers between devices, on_device_small(): far = lax.ppermute(far, 'view', [(v, v ^ 1) for v in range(views)])  0.34 us
  transfers between devices with their start and end apart: 1, of which 1 were waited for; matrix products, arithmetic and copies ran while one was open for 0% of the time, Pallas kernels for 4%

profile of v9, /device:TPU:0, one launch (start us, length us, event | category | flops | bytes accessed | tf_op | source)
XLA Modules:
  0.0 16.0 jit_solution(12111169223704930082)
XLA Ops:
  0.0 0.8 %pack.1 = f32[336,128]{1,0:T(8,128)S(1)} custom-call(s32[1,8]{1,0:T(1,128)} %bitcast.12, f32[8,128]{1,0:T(8,128)} %bitcast.11, f32[16,128]{1,0:T(8,128)} %bitcast.10, f32[1,33]{1,0:T(1,128)} %tx.1, f32[1,33]{1,0:T(1,128)} %ty.1, f32[1,33]{1,0:T(1,128)} %tz.1), custom_call_target="tpu_custom_call" | custom-call | tf_op jit(solution)/shard_map/pack/pallas_call | solution.py:225
  0.8 11.7 %all_to_all.5 = f32[16,21,1,128]{3,2,1,0:T(1,128)S(1)} all-to-all(f32[16,21,1,128]{3,2,1,0:T(1,128)S(1)} %bitcast.8), channel_id=1, replica_groups={{29,2,1,14,17,18,12,28,13,16,15,0,19,30,3,31},{21,10,9,6,25,26,4,20,5,2..., dimensions={0} | all-to-all | bytes 344064 | tf_op jit(solution)/shard_map/all_to_all | solution.py:234
  12.6 0.8 %collective-permute-start = (f32[256,128]{1,0:T(8,128)S(1)}, f32[256,128]{1,0:T(8,128)S(1)}, u32[]{:S(2)}, u32[]{:S(2)}) collective-permute-start(f32[256,128]{1,0:T(8,128)S(1)} %bitcast.9), channel_id=1, source_target_pairs={{0,8},{8,0},{16,24},{24,16},{1,9},{9,1},{17,25},{25,17},{2,10},{10... | collective-permute-start | bytes 393224 | tf_op jit(solution)/shard_map/ppermute | solution.py:238
  13.4 0.6 %prepare.1 = (f32[64,128]{1,0:T(8,128)S(1)}, f32[4,64,128]{2,1,0:T(8,128)S(1)}, f32[4,64,128]{2,1,0:T(8,128)S(1)}, f32[4,64,128]{2,1,0:T(8,128)S(1)}, bf16[384,5...) custom-call(f32[336,128]{1,0:T(8,128)S(1)} %bitcast.7), custom_call_target="tpu_custom_call" | custom-call | tf_op jit(solution)/shard_map/prepare/pallas_call | solution.py:241
  14.0 0.3 %collective-permute-done.far = f32[256,128]{1,0:T(8,128)S(1)} collective-permute-done((f32[256,128]{1,0:T(8,128)S(1)}, f32[256,128]{1,0:T(8,128)S(1)}, u32[]{:S(2)}, u32[]{:S(2)}) %collective-permute-start) | collective-permute-done | bytes 131104 | tf_op jit(solution)/shard_map/ppermute | solution.py:238
  14.4 1.6 %finish.1 = f32[8,128]{1,0:T(8,128)} custom-call(f32[256,128]{1,0:T(8,128)S(1)} %collective-permute-done.far, f32[64,128]{1,0:T(8,128)S(1)} %get-tuple-element.14.est_in, f32[4,64,128]{2,1,0:T(8,128)S(1)} %get-tuple-element.15.inverse, f32[4,64,128]{2,1,0:T(8,128)S(1)} %get-tuple-element.16.slabs_in, f32[4,64,128]{2,1,0:T(8,128)S(1)} %get-tuple-element.17.slots_in, ...), custom_call_target="tpu_custom_call" | custom-call | tf_op jit(solution)/shard_map/finish/pallas_call | solution.py:258
  (1 shorter events, 0.0 us)
Async XLA Ops:
  12.6 1.8 %collective-permute-start = (f32[256,128]{1,0:T(8,128)S(1)}, f32[256,128]{1,0:T(8,128)S(1)}, u32[]{:S(2)}, u32[]{:S(2)}) collective-permute-start(f32[256,128]{1,0:T(8,128)S(1)} %bitcast.9), channel_id=1, source_target_pairs={{0,8},{8,0},{16,24},{24,16},{1,9},{9,1},{17,25},{25,17},{2,10},{10... | collective-permute-start | bytes 393224 | tf_op jit(solution)/shard_map/ppermute | solution.py:238

commit v10 on v9

--- a/solution.py
+++ b/solution.py
@@ -62,12 +62,12 @@
 
 def left(value):
     high, low = halves(value)
-    return jnp.concatenate([high, low, high], axis=1)
+    return jnp.concatenate([high, high, low], axis=1)
 
 
 def right(value):
     high, low = halves(value)
-    return jnp.concatenate([high, high, low], axis=0)
+    return jnp.concatenate([high, low, high], axis=0)
 
 
 def lane_pick(tile, index):

time: 16.2 us -> 16.2 us (level)
  no operation moved by 1% of the time
where the time goes in v10:
time: 16.2 us; the launch traced here: 16 us
  blocking collectives  11.7 us (72%)
  Pallas kernels  3.07 us (19%)
  starting transfers between devices  0.81 us (5%)
  waiting for transfers between devices  0.34 us (2%)
    all_to_all x1, blocking collectives, on_device_small(): lax.all_to_all(packet.reshape(copies, PACKET, 1, LANES), ('view', 'block'...  11.7 us
    pallas_call x1, Pallas kernels, on_device_small(): pl.pallas_call(functools.partial(finish_kernel, groups), out_shape=jax.Sh...  1.6 us
    pallas_call x1, Pallas kernels, on_device_small(): pl.pallas_call(functools.partial(pack_kernel, copies), out_shape=pltpu.VM...  0.83 us
    ppermute x1, starting transfers between devices, on_device_small(): far = lax.ppermute(far, 'view', [(v, v ^ 1) for v in range(views)])  0.81 us
    pallas_call x1, Pallas kernels, on_device_small(): pl.pallas_call(functools.partial(prepare_kernel, groups, width // 2), out...  0.64 us
    ppermute x1, waiting for transfers between devices, on_device_small(): far = lax.ppermute(far, 'view', [(v, v ^ 1) for v in range(views)])  0.34 us
  transfers between devices with their start and end apart: 1, of which 1 were waited for; matrix products, arithmetic and copies ran while one was open for 0% of the time, Pallas kernels for 4%

profile of v10, /device:TPU:0, one launch (start us, length us, event | category | flops | bytes accessed | tf_op | source)
XLA Modules:
  0.0 16.0 jit_solution(13420110294071240966)
XLA Ops:
  0.0 0.8 %pack.1 = f32[336,128]{1,0:T(8,128)S(1)} custom-call(s32[1,8]{1,0:T(1,128)} %bitcast.12, f32[8,128]{1,0:T(8,128)} %bitcast.11, f32[16,128]{1,0:T(8,128)} %bitcast.10, f32[1,33]{1,0:T(1,128)} %tx.1, f32[1,33]{1,0:T(1,128)} %ty.1, f32[1,33]{1,0:T(1,128)} %tz.1), custom_call_target="tpu_custom_call" | custom-call | tf_op jit(solution)/shard_map/pack/pallas_call | solution.py:225
  0.8 11.7 %all_to_all.5 = f32[16,21,1,128]{3,2,1,0:T(1,128)S(1)} all-to-all(f32[16,21,1,128]{3,2,1,0:T(1,128)S(1)} %bitcast.8), channel_id=1, replica_groups={{29,2,1,14,17,18,12,28,13,16,15,0,19,30,3,31},{21,10,9,6,25,26,4,20,5,2..., dimensions={0} | all-to-all | bytes 344064 | tf_op jit(solution)/shard_map/all_to_all | solution.py:234
  12.6 0.8 %collective-permute-start = (f32[256,128]{1,0:T(8,128)S(1)}, f32[256,128]{1,0:T(8,128)S(1)}, u32[]{:S(2)}, u32[]{:S(2)}) collective-permute-start(f32[256,128]{1,0:T(8,128)S(1)} %bitcast.9), channel_id=1, source_target_pairs={{0,8},{8,0},{16,24},{24,16},{1,9},{9,1},{17,25},{25,17},{2,10},{10... | collective-permute-start | bytes 393224 | tf_op jit(solution)/shard_map/ppermute | solution.py:238
  13.4 0.6 %prepare.1 = (f32[64,128]{1,0:T(8,128)S(1)}, f32[4,64,128]{2,1,0:T(8,128)S(1)}, f32[4,64,128]{2,1,0:T(8,128)S(1)}, f32[4,64,128]{2,1,0:T(8,128)S(1)}, bf16[384,5...) custom-call(f32[336,128]{1,0:T(8,128)S(1)} %bitcast.7), custom_call_target="tpu_custom_call" | custom-call | tf_op jit(solution)/shard_map/prepare/pallas_call | solution.py:241
  14.0 0.3 %collective-permute-done.far = f32[256,128]{1,0:T(8,128)S(1)} collective-permute-done((f32[256,128]{1,0:T(8,128)S(1)}, f32[256,128]{1,0:T(8,128)S(1)}, u32[]{:S(2)}, u32[]{:S(2)}) %collective-permute-start) | collective-permute-done | bytes 131104 | tf_op jit(solution)/shard_map/ppermute | solution.py:238
  14.4 1.6 %finish.1 = f32[8,128]{1,0:T(8,128)} custom-call(f32[256,128]{1,0:T(8,128)S(1)} %collective-permute-done.far, f32[64,128]{1,0:T(8,128)S(1)} %get-tuple-element.14.est_in, f32[4,64,128]{2,1,0:T(8,128)S(1)} %get-tuple-element.15.inverse, f32[4,64,128]{2,1,0:T(8,128)S(1)} %get-tuple-element.16.slabs_in, f32[4,64,128]{2,1,0:T(8,128)S(1)} %get-tuple-element.17.slots_in, ...), custom_call_target="tpu_custom_call" | custom-call | tf_op jit(solution)/shard_map/finish/pallas_call | solution.py:258
  (1 shorter events, 0.0 us)
Async XLA Ops:
  12.6 1.8 %collective-permute-start = (f32[256,128]{1,0:T(8,128)S(1)}, f32[256,128]{1,0:T(8,128)S(1)}, u32[]{:S(2)}, u32[]{:S(2)}) collective-permute-start(f32[256,128]{1,0:T(8,128)S(1)} %bitcast.9), channel_id=1, source_target_pairs={{0,8},{8,0},{16,24},{24,16},{1,9},{9,1},{17,25},{25,17},{2,10},{10... | collective-permute-start | bytes 393224 | tf_op jit(solution)/shard_map/ppermute | solution.py:238
